TPU v7x, 256 devices: a whole 4x4x8 slice. The times are simulated.
256 devices in a mesh: site: 16 (over x, y), sector: 16 (over z, core).
Axes of the slice: x: 4, y: 4, z: 8, core: 2. Of those that a mesh axis runs over, the one named last changes fastest.
Arguments:
- boundary: bfloat16 [16, 4096, 32, 256], P('site', 'sector'), may hold values from -0.375 to 0.375
- peps_row: bfloat16 [16, 32, 8], P('site'), may hold values from -1 to 1
- sketch: bfloat16 [16, 4096, 8, 256], P('site', 'sector'), may hold values from -0.125 to 0.125
- charges: int32 [16, 8], P('site'), may hold values from -1 to 1
- left_edge: bfloat16 [512, 4096], P(None, 'sector'), may hold values from -6 to 6
Outputs:
- environments: float32 [16, 512, 4096], P('site', None, 'sector')
Inputs may be any that keep to these rules, and one draw needn't show every extreme that they name: `charges`: each entry is a charge change of -1, 0 or +1.
All inputs are finite; a program needn't handle non-finite values.
Results may differ from a plain program's by a relative error of at most 0.0003.
Values sent between devices are 32-bit elements; how exact they have to be, the bound alone decides.
No kernel may reach another device: no remote copies, remote signals or barrier semaphores. Data moves between devices by JAX's collectives and lax.ppermute only.
A program may use at most 64 MiB of HBM per device.

v0:
```python
import jax
import jax.numpy as jnp
from jax import lax
from jax.sharding import PartitionSpec as P


def with_halo(block, sides, width):
    for axis, dim in sides:
        count = lax.axis_size(axis)
        forward = [(i, i + 1) for i in range(count - 1)]
        backward = [(target, source) for source, target in forward]
        low = lax.ppermute(
            lax.slice_in_dim(block, block.shape[dim] - width, None, axis=dim), axis, forward
        )
        high = lax.ppermute(lax.slice_in_dim(block, 0, width, axis=dim), axis, backward)
        block = jnp.concatenate([low, block, high], axis=dim)
    return block


def passed_along(array, axis, by):
    peers = lax.axis_size(axis)
    pairs = [(i, i + by) for i in range(peers) if 0 <= i + by < peers]
    return lax.ppermute(array, axis, pairs)


def local(boundary, peps_row, sketch, charges, left_edge):
    local_sites = boundary.shape[0]
    block_width = boundary.shape[3]
    total_rows = left_edge.shape[0]
    absorbed = jnp.einsum("jwpv,jpl->jwlv", boundary, peps_row, preferred_element_type=jnp.float32)
    sketch_wide = sketch.astype(jnp.float32)
    onehot = (charges[:, :, None] == jnp.arange(-1, 2, dtype=jnp.int32)[None, None, :]).astype(
        jnp.float32
    )
    site_devices = lax.axis_size("site")
    position = lax.axis_index("site")
    slab_count = 4
    slab_rows = total_rows // slab_count

    def apply_site(state_rows, which):
        grown = jnp.einsum(
            "rw,wlv->rlv", state_rows, absorbed[which], precision=lax.Precision.HIGHEST
        )
        reduced = jnp.einsum(
            "rlv,vlu->rlu", grown, sketch_wide[which], precision=lax.Precision.HIGHEST
        )
        return jnp.einsum("rlu,ls->sru", reduced, onehot[which], precision=lax.Precision.HIGHEST)

    def wave_step(t, state_pair):
        incoming, results = state_pair
        offset = t - position
        active = jnp.logical_and(offset >= 0, offset < slab_count)
        slab_index = jnp.clip(offset, 0, slab_count - 1)
        edge_rows = lax.dynamic_slice_in_dim(
            left_edge, slab_index * slab_rows, slab_rows, 0
        ).astype(jnp.float32)
        state_rows = jnp.where(position == 0, edge_rows, incoming)
        parts = lax.cond(
            active,
            lambda rows_in: apply_site(rows_in, 0),
            lambda rows_in: jnp.zeros((3, slab_rows, block_width), jnp.float32),
            state_rows,
        )
        outflow = jnp.stack([parts[0], parts[2]], axis=0)
        padded = with_halo(outflow, (("sector", 0),), 1)
        state_rows = parts[1] + padded[0] + padded[3]
        current = lax.dynamic_slice(
            results,
            (jnp.int32(0), slab_index * slab_rows, jnp.int32(0)),
            (1, slab_rows, block_width),
        )
        results = lax.dynamic_update_slice(
            results,
            jnp.where(active, state_rows[None], current),
            (jnp.int32(0), slab_index * slab_rows, jnp.int32(0)),
        )
        incoming = passed_along(state_rows, "site", 1)
        return (incoming, results)

    initial = (
        jnp.zeros((slab_rows, block_width), jnp.float32),
        jnp.zeros((local_sites, total_rows, block_width), jnp.float32),
    )
    final_pair = lax.fori_loop(0, slab_count + site_devices - 1, wave_step, initial)
    return final_pair[1]


def solution(mesh):
    in_specs = (
        P("site", "sector", None, None),
        P("site", None, None),
        P("site", "sector", None, None),
        P("site", None),
        P(None, "sector"),
    )
    out_specs = P("site", None, "sector")
    return jax.shard_map(local, mesh=mesh, in_specs=in_specs, out_specs=out_specs, check_vma=False)
```

profile of v0, /device:TPU:126, one launch (start us, length us, event | category | flops | bytes accessed | tf_op | source)
XLA Modules:
  0.0 470.6 jit_solution(8413009200270944826)
XLA Ops:
  6.5 464.1 %while.17 = (s32[]{:T(128)}, f32[128,256]{1,0:T(8,128)S(1)}, f32[1,512,256]{2,1,0:T(8,128)}, s32[]{:T(128)}, bf16[512,256]{1,0:T(8,128)(2,1)}, /*index=5*/pred[]...) while((s32[]{:T(128)}, f32[128,256]{1,0:T(8,128)S(1)}, ...), condition=%wide.region_3.4_spmd.clone, body=%wide.region_0.3_spmd.clone.sunk | while | flops 1620213760 | bytes 12911275 | solution.py:84
  18.3 6.1 %collective-permute-done.2 = f32[128,256]{1,0:T(8,128)S(1)} collective-permute-done((f32[128,256]{1,0:T(8,128)S(1)}, f32[128,256]{1,0:T(8,128)S(1)}, u32[]{:S(2)}, u32[]{:S(2)}) %collective-permute-start.2) | collective-permute-done | bytes 131104 | tf_op jit(solution)/shard_map/while/body/eval_jaxpr/ppermute | solution.py:23
  36.3 6.1 %collective-permute-done.2 = f32[128,256]{1,0:T(8,128)S(1)} collective-permute-done((f32[128,256]{1,0:T(8,128)S(1)}, f32[128,256]{1,0:T(8,128)S(1)}, u32[]{:S(2)}, u32[]{:S(2)}) %collective-permute-start.2) | collective-permute-done | bytes 131104 | tf_op jit(solution)/shard_map/while/body/eval_jaxpr/ppermute | solution.py:23
  54.2 6.1 %collective-permute-done.2 = f32[128,256]{1,0:T(8,128)S(1)} collective-permute-done((f32[128,256]{1,0:T(8,128)S(1)}, f32[128,256]{1,0:T(8,128)S(1)}, u32[]{:S(2)}, u32[]{:S(2)}) %collective-permute-start.2) | collective-permute-done | bytes 131104 | tf_op jit(solution)/shard_map/while/body/eval_jaxpr/ppermute | solution.py:23
  72.1 6.1 %collective-permute-done.2 = f32[128,256]{1,0:T(8,128)S(1)} collective-permute-done((f32[128,256]{1,0:T(8,128)S(1)}, f32[128,256]{1,0:T(8,128)S(1)}, u32[]{:S(2)}, u32[]{:S(2)}) %collective-permute-start.2) | collective-permute-done | bytes 131104 | tf_op jit(solution)/shard_map/while/body/eval_jaxpr/ppermute | solution.py:23
  90.0 6.3 %collective-permute-done.2 = f32[128,256]{1,0:T(8,128)S(1)} collective-permute-done((f32[128,256]{1,0:T(8,128)S(1)}, f32[128,256]{1,0:T(8,128)S(1)}, u32[]{:S(2)}, u32[]{:S(2)}) %collective-permute-start.2) | collective-permute-done | bytes 131104 | tf_op jit(solution)/shard_map/while/body/eval_jaxpr/ppermute | solution.py:23
  108.2 8.2 %collective-permute-done.2 = f32[128,256]{1,0:T(8,128)S(1)} collective-permute-done((f32[128,256]{1,0:T(8,128)S(1)}, f32[128,256]{1,0:T(8,128)S(1)}, u32[]{:S(2)}, u32[]{:S(2)}) %collective-permute-start.2) | collective-permute-done | bytes 131104 | tf_op jit(solution)/shard_map/while/body/eval_jaxpr/ppermute | solution.py:23
  128.2 8.2 %collective-permute-done.2 = f32[128,256]{1,0:T(8,128)S(1)} collective-permute-done((f32[128,256]{1,0:T(8,128)S(1)}, f32[128,256]{1,0:T(8,128)S(1)}, u32[]{:S(2)}, u32[]{:S(2)}) %collective-permute-start.2) | collective-permute-done | bytes 131104 | tf_op jit(solution)/shard_map/while/body/eval_jaxpr/ppermute | solution.py:23
  148.2 8.2 %collective-permute-done.2 = f32[128,256]{1,0:T(8,128)S(1)} collective-permute-done((f32[128,256]{1,0:T(8,128)S(1)}, f32[128,256]{1,0:T(8,128)S(1)}, u32[]{:S(2)}, u32[]{:S(2)}) %collective-permute-start.2) | collective-permute-done | bytes 131104 | tf_op jit(solution)/shard_map/while/body/eval_jaxpr/ppermute | solution.py:23
  168.3 8.2 %collective-permute-done.2 = f32[128,256]{1,0:T(8,128)S(1)} collective-permute-done((f32[128,256]{1,0:T(8,128)S(1)}, f32[128,256]{1,0:T(8,128)S(1)}, u32[]{:S(2)}, u32[]{:S(2)}) %collective-permute-start.2) | collective-permute-done | bytes 131104 | tf_op jit(solution)/shard_map/while/body/eval_jaxpr/ppermute | solution.py:23
  188.3 8.2 %collective-permute-done.2 = f32[128,256]{1,0:T(8,128)S(1)} collective-permute-done((f32[128,256]{1,0:T(8,128)S(1)}, f32[128,256]{1,0:T(8,128)S(1)}, u32[]{:S(2)}, u32[]{:S(2)}) %collective-permute-start.2) | collective-permute-done | bytes 131104 | tf_op jit(solution)/shard_map/while/body/eval_jaxpr/ppermute | solution.py:23
  208.3 8.2 %collective-permute-done.2 = f32[128,256]{1,0:T(8,128)S(1)} collective-permute-done((f32[128,256]{1,0:T(8,128)S(1)}, f32[128,256]{1,0:T(8,128)S(1)}, u32[]{:S(2)}, u32[]{:S(2)}) %collective-permute-start.2) | collective-permute-done | bytes 131104 | tf_op jit(solution)/shard_map/while/body/eval_jaxpr/ppermute | solution.py:23
  228.3 8.2 %collective-permute-done.2 = f32[128,256]{1,0:T(8,128)S(1)} collective-permute-done((f32[128,256]{1,0:T(8,128)S(1)}, f32[128,256]{1,0:T(8,128)S(1)}, u32[]{:S(2)}, u32[]{:S(2)}) %collective-permute-start.2) | collective-permute-done | bytes 131104 | tf_op jit(solution)/shard_map/while/body/eval_jaxpr/ppermute | solution.py:23
  248.4 8.2 %collective-permute-done.2 = f32[128,256]{1,0:T(8,128)S(1)} collective-permute-done((f32[128,256]{1,0:T(8,128)S(1)}, f32[128,256]{1,0:T(8,128)S(1)}, u32[]{:S(2)}, u32[]{:S(2)}) %collective-permute-start.2) | collective-permute-done | bytes 131104 | tf_op jit(solution)/shard_map/while/body/eval_jaxpr/ppermute | solution.py:23
  268.4 8.2 %collective-permute-done.2 = f32[128,256]{1,0:T(8,128)S(1)} collective-permute-done((f32[128,256]{1,0:T(8,128)S(1)}, f32[128,256]{1,0:T(8,128)S(1)}, u32[]{:S(2)}, u32[]{:S(2)}) %collective-permute-start.2) | collective-permute-done | bytes 131104 | tf_op jit(solution)/shard_map/while/body/eval_jaxpr/ppermute | solution.py:23
  288.4 76.5 %collective-permute-done.2 = f32[128,256]{1,0:T(8,128)S(1)} collective-permute-done((f32[128,256]{1,0:T(8,128)S(1)}, f32[128,256]{1,0:T(8,128)S(1)}, u32[]{:S(2)}, u32[]{:S(2)}) %collective-permute-start.2) | collective-permute-done | bytes 131104 | tf_op jit(solution)/shard_map/while/body/eval_jaxpr/ppermute | solution.py:23
  365.8 7.0 %conditional.3 = (f32[3,128,256]{2,0,1:T(4,128)S(1)}) conditional(s32[]{:T(128)} %convert_element_type.45, () %tuple.51, (pred[]{:T(512)}, f32[128,256]{1,0:T(8,128)S(1)}, f32[128,256]{1,0:T(8,128)S(1)}, f32[1,256,8,256]{3,2,1,0:T(8,128)}, f32[1,256,8,256]{3,2,1,0:T(8,128)S(1)}, /*index=5*/f32[1,8,3]{1,2,0:T(4,128)S(1)}) %tuple.52), branch_computations={%region_1.1_spmd, %region_2.2_spmd} | conditional | flops 1620082688 | bytes 9044073 | solution.py:58
  383.7 8.3 %collective-permute-done.2 = f32[128,256]{1,0:T(8,128)S(1)} collective-permute-done((f32[128,256]{1,0:T(8,128)S(1)}, f32[128,256]{1,0:T(8,128)S(1)}, u32[]{:S(2)}, u32[]{:S(2)}) %collective-permute-start.2) | collective-permute-done | bytes 131104 | tf_op jit(solution)/shard_map/while/body/eval_jaxpr/ppermute | solution.py:23
  392.9 7.0 %conditional.3 = (f32[3,128,256]{2,0,1:T(4,128)S(1)}) conditional(s32[]{:T(128)} %convert_element_type.45, () %tuple.51, (pred[]{:T(512)}, f32[128,256]{1,0:T(8,128)S(1)}, f32[128,256]{1,0:T(8,128)S(1)}, f32[1,256,8,256]{3,2,1,0:T(8,128)}, f32[1,256,8,256]{3,2,1,0:T(8,128)S(1)}, /*index=5*/f32[1,8,3]{1,2,0:T(4,128)S(1)}) %tuple.52), branch_computations={%region_1.1_spmd, %region_2.2_spmd} | conditional | flops 1620082688 | bytes 9044073 | solution.py:58
  410.8 8.2 %collective-permute-done.2 = f32[128,256]{1,0:T(8,128)S(1)} collective-permute-done((f32[128,256]{1,0:T(8,128)S(1)}, f32[128,256]{1,0:T(8,128)S(1)}, u32[]{:S(2)}, u32[]{:S(2)}) %collective-permute-start.2) | collective-permute-done | bytes 131104 | tf_op jit(solution)/shard_map/while/body/eval_jaxpr/ppermute | solution.py:23
  419.9 7.0 %conditional.3 = (f32[3,128,256]{2,0,1:T(4,128)S(1)}) conditional(s32[]{:T(128)} %convert_element_type.45, () %tuple.51, (pred[]{:T(512)}, f32[128,256]{1,0:T(8,128)S(1)}, f32[128,256]{1,0:T(8,128)S(1)}, f32[1,256,8,256]{3,2,1,0:T(8,128)}, f32[1,256,8,256]{3,2,1,0:T(8,128)S(1)}, /*index=5*/f32[1,8,3]{1,2,0:T(4,128)S(1)}) %tuple.52), branch_computations={%region_1.1_spmd, %region_2.2_spmd} | conditional | flops 1620082688 | bytes 9044073 | solution.py:58
  437.8 8.2 %collective-permute-done.2 = f32[128,256]{1,0:T(8,128)S(1)} collective-permute-done((f32[128,256]{1,0:T(8,128)S(1)}, f32[128,256]{1,0:T(8,128)S(1)}, u32[]{:S(2)}, u32[]{:S(2)}) %collective-permute-start.2) | collective-permute-done | bytes 131104 | tf_op jit(solution)/shard_map/while/body/eval_jaxpr/ppermute | solution.py:23
  446.9 7.0 %conditional.3 = (f32[3,128,256]{2,0,1:T(4,128)S(1)}) conditional(s32[]{:T(128)} %convert_element_type.45, () %tuple.51, (pred[]{:T(512)}, f32[128,256]{1,0:T(8,128)S(1)}, f32[128,256]{1,0:T(8,128)S(1)}, f32[1,256,8,256]{3,2,1,0:T(8,128)}, f32[1,256,8,256]{3,2,1,0:T(8,128)S(1)}, /*index=5*/f32[1,8,3]{1,2,0:T(4,128)S(1)}) %tuple.52), branch_computations={%region_1.1_spmd, %region_2.2_spmd} | conditional | flops 1620082688 | bytes 9044073 | solution.py:58
  464.8 5.8 %collective-permute-done.2 = f32[128,256]{1,0:T(8,128)S(1)} collective-permute-done((f32[128,256]{1,0:T(8,128)S(1)}, f32[128,256]{1,0:T(8,128)S(1)}, u32[]{:S(2)}, u32[]{:S(2)}) %collective-permute-start.2) | collective-permute-done | bytes 131104 | tf_op jit(solution)/shard_map/while/body/eval_jaxpr/ppermute | solution.py:23
  (279 shorter events, 258.5 us)
Async XLA Ops:
  9.7 6.3 %collective-permute-start.1 = (f32[1,128,256]{2,0,1:T(1,128)S(1)}, f32[1,128,256]{2,0,1:T(1,128)S(1)}, u32[]{:S(2)}, u32[]{:S(2)}) collective-permute-start(f32[1,128,256]{2,0,1:T(1,128)S(1)} %get-tuple-element.324), channel_id=1, source_target_pairs={{0,1},{1,2},{2,3},{3,4},{4,5},{5,6},{6,7},{7,8},{8,9},{9,10},{10,1... | collective-permute-start | bytes 393224 | tf_op jit(solution)/shard_map/while/body/eval_jaxpr/ppermute | solution.py:12
  16.4 8.1 %collective-permute-start.2 = (f32[128,256]{1,0:T(8,128)S(1)}, f32[128,256]{1,0:T(8,128)S(1)}, u32[]{:S(2)}, u32[]{:S(2)}) collective-permute-start(f32[128,256]{1,0:T(8,128)S(1)} %bitcast.36), channel_id=1, source_target_pairs={{0,16},{16,32},{32,48},{48,64},{64,80},{80,96},{96,112},{112,128},... | collective-permute-start | bytes 393224 | tf_op jit(solution)/shard_map/while/body/eval_jaxpr/ppermute | solution.py:23
  27.6 6.3 %collective-permute-start.1 = (f32[1,128,256]{2,0,1:T(1,128)S(1)}, f32[1,128,256]{2,0,1:T(1,128)S(1)}, u32[]{:S(2)}, u32[]{:S(2)}) collective-permute-start(f32[1,128,256]{2,0,1:T(1,128)S(1)} %get-tuple-element.324), channel_id=1, source_target_pairs={{0,1},{1,2},{2,3},{3,4},{4,5},{5,6},{6,7},{7,8},{8,9},{9,10},{10,1... | collective-permute-start | bytes 393224 | tf_op jit(solution)/shard_map/while/body/eval_jaxpr/ppermute | solution.py:12
  34.3 8.1 %collective-permute-start.2 = (f32[128,256]{1,0:T(8,128)S(1)}, f32[128,256]{1,0:T(8,128)S(1)}, u32[]{:S(2)}, u32[]{:S(2)}) collective-permute-start(f32[128,256]{1,0:T(8,128)S(1)} %bitcast.36), channel_id=1, source_target_pairs={{0,16},{16,32},{32,48},{48,64},{64,80},{80,96},{96,112},{112,128},... | collective-permute-start | bytes 393224 | tf_op jit(solution)/shard_map/while/body/eval_jaxpr/ppermute | solution.py:23
  45.5 6.3 %collective-permute-start.1 = (f32[1,128,256]{2,0,1:T(1,128)S(1)}, f32[1,128,256]{2,0,1:T(1,128)S(1)}, u32[]{:S(2)}, u32[]{:S(2)}) collective-permute-start(f32[1,128,256]{2,0,1:T(1,128)S(1)} %get-tuple-element.324), channel_id=1, source_target_pairs={{0,1},{1,2},{2,3},{3,4},{4,5},{5,6},{6,7},{7,8},{8,9},{9,10},{10,1... | collective-permute-start | bytes 393224 | tf_op jit(solution)/shard_map/while/body/eval_jaxpr/ppermute | solution.py:12
  52.2 8.1 %collective-permute-start.2 = (f32[128,256]{1,0:T(8,128)S(1)}, f32[128,256]{1,0:T(8,128)S(1)}, u32[]{:S(2)}, u32[]{:S(2)}) collective-permute-start(f32[128,256]{1,0:T(8,128)S(1)} %bitcast.36), channel_id=1, source_target_pairs={{0,16},{16,32},{32,48},{48,64},{64,80},{80,96},{96,112},{112,128},... | collective-permute-start | bytes 393224 | tf_op jit(solution)/shard_map/while/body/eval_jaxpr/ppermute | solution.py:23
  63.4 6.3 %collective-permute-start.1 = (f32[1,128,256]{2,0,1:T(1,128)S(1)}, f32[1,128,256]{2,0,1:T(1,128)S(1)}, u32[]{:S(2)}, u32[]{:S(2)}) collective-permute-start(f32[1,128,256]{2,0,1:T(1,128)S(1)} %get-tuple-element.324), channel_id=1, source_target_pairs={{0,1},{1,2},{2,3},{3,4},{4,5},{5,6},{6,7},{7,8},{8,9},{9,10},{10,1... | collective-permute-start | bytes 393224 | tf_op jit(solution)/shard_map/while/body/eval_jaxpr/ppermute | solution.py:12
  70.1 8.1 %collective-permute-start.2 = (f32[128,256]{1,0:T(8,128)S(1)}, f32[128,256]{1,0:T(8,128)S(1)}, u32[]{:S(2)}, u32[]{:S(2)}) collective-permute-start(f32[128,256]{1,0:T(8,128)S(1)} %bitcast.36), channel_id=1, source_target_pairs={{0,16},{16,32},{32,48},{48,64},{64,80},{80,96},{96,112},{112,128},... | collective-permute-start | bytes 393224 | tf_op jit(solution)/shard_map/while/body/eval_jaxpr/ppermute | solution.py:23
  88.1 8.3 %collective-permute-start.2 = (f32[128,256]{1,0:T(8,128)S(1)}, f32[128,256]{1,0:T(8,128)S(1)}, u32[]{:S(2)}, u32[]{:S(2)}) collective-permute-start(f32[128,256]{1,0:T(8,128)S(1)} %bitcast.36), channel_id=1, source_target_pairs={{0,16},{16,32},{32,48},{48,64},{64,80},{80,96},{96,112},{112,128},... | collective-permute-start | bytes 393224 | tf_op jit(solution)/shard_map/while/body/eval_jaxpr/ppermute | solution.py:23
  106.2 10.2 %collective-permute-start.2 = (f32[128,256]{1,0:T(8,128)S(1)}, f32[128,256]{1,0:T(8,128)S(1)}, u32[]{:S(2)}, u32[]{:S(2)}) collective-permute-start(f32[128,256]{1,0:T(8,128)S(1)} %bitcast.36), channel_id=1, source_target_pairs={{0,16},{16,32},{32,48},{48,64},{64,80},{80,96},{96,112},{112,128},... | collective-permute-start | bytes 393224 | tf_op jit(solution)/shard_map/while/body/eval_jaxpr/ppermute | solution.py:23
  126.2 10.2 %collective-permute-start.2 = (f32[128,256]{1,0:T(8,128)S(1)}, f32[128,256]{1,0:T(8,128)S(1)}, u32[]{:S(2)}, u32[]{:S(2)}) collective-permute-start(f32[128,256]{1,0:T(8,128)S(1)} %bitcast.36), channel_id=1, source_target_pairs={{0,16},{16,32},{32,48},{48,64},{64,80},{80,96},{96,112},{112,128},... | collective-permute-start | bytes 393224 | tf_op jit(solution)/shard_map/while/body/eval_jaxpr/ppermute | solution.py:23
  146.2 10.2 %collective-permute-start.2 = (f32[128,256]{1,0:T(8,128)S(1)}, f32[128,256]{1,0:T(8,128)S(1)}, u32[]{:S(2)}, u32[]{:S(2)}) collective-permute-start(f32[128,256]{1,0:T(8,128)S(1)} %bitcast.36), channel_id=1, source_target_pairs={{0,16},{16,32},{32,48},{48,64},{64,80},{80,96},{96,112},{112,128},... | collective-permute-start | bytes 393224 | tf_op jit(solution)/shard_map/while/body/eval_jaxpr/ppermute | solution.py:23
  166.3 10.2 %collective-permute-start.2 = (f32[128,256]{1,0:T(8,128)S(1)}, f32[128,256]{1,0:T(8,128)S(1)}, u32[]{:S(2)}, u32[]{:S(2)}) collective-permute-start(f32[128,256]{1,0:T(8,128)S(1)} %bitcast.36), channel_id=1, source_target_pairs={{0,16},{16,32},{32,48},{48,64},{64,80},{80,96},{96,112},{112,128},... | collective-permute-start | bytes 393224 | tf_op jit(solution)/shard_map/while/body/eval_jaxpr/ppermute | solution.py:23
  186.3 10.2 %collective-permute-start.2 = (f32[128,256]{1,0:T(8,128)S(1)}, f32[128,256]{1,0:T(8,128)S(1)}, u32[]{:S(2)}, u32[]{:S(2)}) collective-permute-start(f32[128,256]{1,0:T(8,128)S(1)} %bitcast.36), channel_id=1, source_target_pairs={{0,16},{16,32},{32,48},{48,64},{64,80},{80,96},{96,112},{112,128},... | collective-permute-start | bytes 393224 | tf_op jit(solution)/shard_map/while/body/eval_jaxpr/ppermute | solution.py:23
  206.3 10.2 %collective-permute-start.2 = (f32[128,256]{1,0:T(8,128)S(1)}, f32[128,256]{1,0:T(8,128)S(1)}, u32[]{:S(2)}, u32[]{:S(2)}) collective-permute-start(f32[128,256]{1,0:T(8,128)S(1)} %bitcast.36), channel_id=1, source_target_pairs={{0,16},{16,32},{32,48},{48,64},{64,80},{80,96},{96,112},{112,128},... | collective-permute-start | bytes 393224 | tf_op jit(solution)/shard_map/while/body/eval_jaxpr/ppermute | solution.py:23
  226.4 10.2 %collective-permute-start.2 = (f32[128,256]{1,0:T(8,128)S(1)}, f32[128,256]{1,0:T(8,128)S(1)}, u32[]{:S(2)}, u32[]{:S(2)}) collective-permute-start(f32[128,256]{1,0:T(8,128)S(1)} %bitcast.36), channel_id=1, source_target_pairs={{0,16},{16,32},{32,48},{48,64},{64,80},{80,96},{96,112},{112,128},... | collective-permute-start | bytes 393224 | tf_op jit(solution)/shard_map/while/body/eval_jaxpr/ppermute | solution.py:23
  246.4 10.2 %collective-permute-start.2 = (f32[128,256]{1,0:T(8,128)S(1)}, f32[128,256]{1,0:T(8,128)S(1)}, u32[]{:S(2)}, u32[]{:S(2)}) collective-permute-start(f32[128,256]{1,0:T(8,128)S(1)} %bitcast.36), channel_id=1, source_target_pairs={{0,16},{16,32},{32,48},{48,64},{64,80},{80,96},{96,112},{112,128},... | collective-permute-start | bytes 393224 | tf_op jit(solution)/shard_map/while/body/eval_jaxpr/ppermute | solution.py:23
  266.4 10.2 %collective-permute-start.2 = (f32[128,256]{1,0:T(8,128)S(1)}, f32[128,256]{1,0:T(8,128)S(1)}, u32[]{:S(2)}, u32[]{:S(2)}) collective-permute-start(f32[128,256]{1,0:T(8,128)S(1)} %bitcast.36), channel_id=1, source_target_pairs={{0,16},{16,32},{32,48},{48,64},{64,80},{80,96},{96,112},{112,128},... | collective-permute-start | bytes 393224 | tf_op jit(solution)/shard_map/while/body/eval_jaxpr/ppermute | solution.py:23
  286.5 78.4 %collective-permute-start.2 = (f32[128,256]{1,0:T(8,128)S(1)}, f32[128,256]{1,0:T(8,128)S(1)}, u32[]{:S(2)}, u32[]{:S(2)}) collective-permute-start(f32[128,256]{1,0:T(8,128)S(1)} %bitcast.36), channel_id=1, source_target_pairs={{0,16},{16,32},{32,48},{48,64},{64,80},{80,96},{96,112},{112,128},... | collective-permute-start | bytes 393224 | tf_op jit(solution)/shard_map/while/body/eval_jaxpr/ppermute | solution.py:23
  381.7 10.3 %collective-permute-start.2 = (f32[128,256]{1,0:T(8,128)S(1)}, f32[128,256]{1,0:T(8,128)S(1)}, u32[]{:S(2)}, u32[]{:S(2)}) collective-permute-start(f32[128,256]{1,0:T(8,128)S(1)} %bitcast.36), channel_id=1, source_target_pairs={{0,16},{16,32},{32,48},{48,64},{64,80},{80,96},{96,112},{112,128},... | collective-permute-start | bytes 393224 | tf_op jit(solution)/shard_map/while/body/eval_jaxpr/ppermute | solution.py:23
  408.8 10.2 %collective-permute-start.2 = (f32[128,256]{1,0:T(8,128)S(1)}, f32[128,256]{1,0:T(8,128)S(1)}, u32[]{:S(2)}, u32[]{:S(2)}) collective-permute-start(f32[128,256]{1,0:T(8,128)S(1)} %bitcast.36), channel_id=1, source_target_pairs={{0,16},{16,32},{32,48},{48,64},{64,80},{80,96},{96,112},{112,128},... | collective-permute-start | bytes 393224 | tf_op jit(solution)/shard_map/while/body/eval_jaxpr/ppermute | solution.py:23
  435.8 10.2 %collective-permute-start.2 = (f32[128,256]{1,0:T(8,128)S(1)}, f32[128,256]{1,0:T(8,128)S(1)}, u32[]{:S(2)}, u32[]{:S(2)}) collective-permute-start(f32[128,256]{1,0:T(8,128)S(1)} %bitcast.36), channel_id=1, source_target_pairs={{0,16},{16,32},{32,48},{48,64},{64,80},{80,96},{96,112},{112,128},... | collective-permute-start | bytes 393224 | tf_op jit(solution)/shard_map/while/body/eval_jaxpr/ppermute | solution.py:23
  456.1 6.3 %collective-permute-start.1 = (f32[1,128,256]{2,0,1:T(1,128)S(1)}, f32[1,128,256]{2,0,1:T(1,128)S(1)}, u32[]{:S(2)}, u32[]{:S(2)}) collective-permute-start(f32[1,128,256]{2,0,1:T(1,128)S(1)} %get-tuple-element.324), channel_id=1, source_target_pairs={{0,1},{1,2},{2,3},{3,4},{4,5},{5,6},{6,7},{7,8},{8,9},{9,10},{10,1... | collective-permute-start | bytes 393224 | tf_op jit(solution)/shard_map/while/body/eval_jaxpr/ppermute | solution.py:12
  462.8 7.8 %collective-permute-start.2 = (f32[128,256]{1,0:T(8,128)S(1)}, f32[128,256]{1,0:T(8,128)S(1)}, u32[]{:S(2)}, u32[]{:S(2)}) collective-permute-start(f32[128,256]{1,0:T(8,128)S(1)} %bitcast.36), channel_id=1, source_target_pairs={{0,16},{16,32},{32,48},{48,64},{64,80},{80,96},{96,112},{112,128},... | collective-permute-start | bytes 393224 | tf_op jit(solution)/shard_map/while/body/eval_jaxpr/ppermute | solution.py:23
  (35 other events, 194.6 us)
where the time goes:
time: 474 us; the launch traced here: 471 us
  waiting for transfers between devices  268 us (57%)
  starting transfers between devices  107 us (23%)
  local copies, waits for them, and re-layouts  36.2 us (8%)
  matrix products  32.2 us (7%)
  other arithmetic  26.4 us (6%)
    ppermute x19, waiting for transfers between devices, passed_along(): return lax.ppermute(array, axis, pairs)  212 us
    ppermute x19, waiting for transfers between devices, with_halo(): lax.ppermute(lax.slice_in_dim(block, block.shape[dim] - width, None, axis...  55.8 us
    ppermute x19, starting transfers between devices, with_halo(): lax.ppermute(lax.slice_in_dim(block, block.shape[dim] - width, None, axis...  45.7 us
    ppermute x19, starting transfers between devices, with_halo(): lax.ppermute(lax.slice_in_dim(block, 0, width, axis=dim), axis, backward)  36.5 us
    ppermute x19, starting transfers between devices, passed_along(): return lax.ppermute(array, axis, pairs)  24.5 us
    dynamic_slice x19, local copies, waits for them, and re-layouts, wave_step(): lax.dynamic_slice(results, (jnp.int32(0), slab_index * slab_rows, jnp.int...  17.5 us
    convert_element_type x19, other arithmetic, wave_step(): edge_rows = lax.dynamic_slice_in_dim(left_edge, slab_index * slab_rows, s...  16.1 us
    dot_general x4, matrix products, apply_site(): jnp.einsum('rw,wlv->rlv', state_rows, absorbed[which], precision=lax.Prec...  13.6 us
  transfers between devices with their start and end apart: 57, of which 38 were waited for; matrix products, arithmetic and copies ran while one was open for 6% of the time, Pallas kernels for 0%

commit v1 on v0

v1 whole, which is shorter than its diff:
```python
import functools

import jax
import jax.numpy as jnp
from jax import lax
from jax.experimental import pallas as pl
from jax.experimental.pallas import tpu as pltpu
from jax.sharding import PartitionSpec as P

GROUP = 4
CHARGES = 3
LANES = 128


def dot(a, b):
    return jnp.dot(a, b, preferred_element_type=jnp.float32)


def split(x):
    high = x.astype(jnp.bfloat16)
    return high, (x - high.astype(jnp.float32)).astype(jnp.bfloat16)


def transfer_kernel(charge_ref, sign_ref, peps_ref, boundary_ref, sketch_ref,
                    top_ref, bottom_ref, spread, absorbed, wide, total):
    width = total.shape[1]
    phys, bonds = peps_ref.shape
    per = width // phys
    step = pl.program_id(0)
    chunks = boundary_ref.shape[0] // width

    @pl.when(step == 0)
    def _():
        for lane in range(width // LANES):
            wide[lane] = sketch_ref[:, lane * LANES:(lane + 1) * LANES].astype(jnp.float32)
        row = lax.broadcasted_iota(jnp.int32, (phys, width), 0)
        col = lax.broadcasted_iota(jnp.int32, (phys, width), 1)
        tiled = jnp.where(lax.rem(col, phys) == row, 1.0, 0.0).astype(jnp.bfloat16)
        repeated = lax.dot_general(
            peps_ref[...], tiled, (((0,), (0,)), ((), ())), preferred_element_type=jnp.float32
        )
        rows = bonds * per
        pick_row = lax.broadcasted_iota(jnp.int32, (rows, bonds), 0)
        pick_col = lax.broadcasted_iota(jnp.int32, (rows, bonds), 1)
        pick = jnp.where(lax.div(pick_row, per) == pick_col, 1.0, 0.0).astype(jnp.bfloat16)
        spread_rows = dot(pick, repeated.astype(jnp.bfloat16))
        out_row = lax.broadcasted_iota(jnp.int32, (rows, width), 0)
        out_col = lax.broadcasted_iota(jnp.int32, (rows, width), 1)
        keep = lax.rem(out_row, per) == lax.div(out_col, phys)
        spread[...] = jnp.where(keep, spread_rows, 0.0).astype(jnp.bfloat16)

    for chunk in range(chunks):
        piece = dot(spread[...], boundary_ref[chunk * width:(chunk + 1) * width, :])
        at = (step * chunks + chunk) * per
        for bond in range(bonds):
            absorbed[bond, pl.ds(pl.multiple_of(at, per), per), :] = piece[bond * per:(bond + 1) * per]

    @pl.when(step == pl.num_programs(0) - 1)
    def _():
        total[...] = jnp.zeros_like(total)
        for bond in range(bonds):
            high, low = split(absorbed[bond])
            lanes = [wide[lane, pl.ds(bond, width, stride=bonds), :] for lane in range(width // LANES)]
            part = jnp.concatenate(lanes, axis=1).astype(jnp.bfloat16)
            both = dot(jnp.concatenate([high, low], axis=0), part)
            slot = 1 + charge_ref[bond] * sign_ref[0]
            where = pl.ds(pl.multiple_of(slot * width, width), width)
            total[where, :] += both[:width] + both[width:]
        half = total.shape[0] // 2
        top_ref[...] = total[:half]
        bottom_ref[...] = total[half:]


def transfer(boundary, peps_row, sketch, charges, sign):
    width = boundary.shape[3]
    phys, bonds = peps_row.shape[1:]
    flat = boundary.reshape(width * phys, width)
    steps = 8
    half = jax.ShapeDtypeStruct((CHARGES * width // 2, width), jnp.float32)
    whole = lambda shape: pl.BlockSpec(shape, lambda i: (0,) * len(shape))
    return pl.pallas_call(
        transfer_kernel,
        grid=(steps,),
        out_shape=(half, half),
        in_specs=[
            pl.BlockSpec(memory_space=pltpu.SMEM),
            pl.BlockSpec(memory_space=pltpu.SMEM),
            whole((phys, bonds)),
            pl.BlockSpec((width * phys // steps, width), lambda i: (i, 0)),
            whole((width * bonds, width)),
        ],
        out_specs=(whole(half.shape), whole(half.shape)),
        scratch_shapes=[
            pltpu.VMEM((bonds * width // phys, width), jnp.bfloat16),
            pltpu.VMEM((bonds, width, width), jnp.float32),
            pltpu.VMEM((width // LANES, width * bonds, LANES), jnp.float32),
            pltpu.VMEM((CHARGES * width, width), jnp.float32),
        ],
        compiler_params=pltpu.CompilerParams(vmem_limit_bytes=32 * 2**20),
        name="transfer",
    )(charges[0], sign, peps_row[0], flat, sketch.reshape(width * bonds, width))


def load_transfer(which_ref, pieces, high_ref, low_ref, buffer, sem):
    half = buffer.shape[0] // 2
    for k in range(GROUP):
        @pl.when(which_ref[0] == k)
        def _():
            pltpu.make_async_copy(pieces[2 * k], buffer.at[pl.ds(0, half)], sem).start()
            pltpu.make_async_copy(pieces[2 * k + 1], buffer.at[pl.ds(half, half)], sem).start()
    pltpu.make_async_copy(buffer, buffer, sem).wait()
    high, low = split(buffer[...])
    high_ref[...] = high
    low_ref[...] = low


def prepare_kernel(which_ref, *refs):
    load_transfer(which_ref, refs[:8], *refs[8:])


def times(state, high, low):
    rows = state.shape[0]
    state_high, state_low = split(state)
    first = dot(jnp.concatenate([state_high, state_low], axis=0), high)
    return first[:rows] + first[rows:] + dot(state_high, low)


VMEM = pl.BlockSpec(memory_space=pltpu.VMEM)
SMEM = pl.BlockSpec(memory_space=pltpu.SMEM)
ANY = pl.BlockSpec(memory_space=pl.ANY)


def prepare(which, pieces):
    rows, width = pieces[0].shape
    out = jax.ShapeDtypeStruct((2 * rows, width), jnp.bfloat16)
    return pl.pallas_call(
        prepare_kernel,
        out_shape=(out, out),
        in_specs=[SMEM] + [ANY] * 8,
        out_specs=(VMEM, VMEM),
        scratch_shapes=[pltpu.VMEM((2 * rows, width), jnp.float32), pltpu.SemaphoreType.DMA],
        cost_estimate=pl.CostEstimate(flops=0, bytes_accessed=12 * rows * width * 2, transcendentals=0),
        name="prepare",
    )(which, *pieces)


def away_of(state, high_ref, low_ref, out_a, out_b):
    width = state.shape[1]
    out_b[...] = times(state, high_ref[:width], low_ref[:width])
    out_a[...] = times(state, high_ref[2 * width:], low_ref[2 * width:])


def away_kernel(state_ref, high_ref, low_ref, out_a, out_b):
    away_of(state_ref[...], high_ref, low_ref, out_a, out_b)


def summed(edge_ref, stay_ref, from_a, from_b):
    keep = edge_ref[0] == 0
    return stay_ref[...] + from_a[...] + jnp.where(keep, from_b[...], 0.0)


def sum_away_kernel(edge_ref, stay_ref, from_a, from_b, high_ref, low_ref, state_ref, out_a, out_b):
    state = summed(edge_ref, stay_ref, from_a, from_b)
    state_ref[...] = state
    away_of(state, high_ref, low_ref, out_a, out_b)


def sum_kernel(edge_ref, stay_ref, from_a, from_b, state_ref):
    state_ref[...] = summed(edge_ref, stay_ref, from_a, from_b)


def stay_kernel(state_ref, high_ref, low_ref, out_ref):
    width = state_ref.shape[1]
    out_ref[...] = times(state_ref[...], high_ref[width:2 * width], low_ref[width:2 * width])


def call(kernel, outs, smem, arrays, tiles, name):
    shape = jax.ShapeDtypeStruct(arrays[0].shape, jnp.float32)
    rows, width = shape.shape
    flops = 2 * 3 * tiles * rows * width * width
    moved = sum(a.size * a.dtype.itemsize for a in arrays) + 4 * outs * rows * width
    return pl.pallas_call(
        kernel,
        out_shape=(shape,) * outs if outs > 1 else shape,
        in_specs=[SMEM] * len(smem) + [VMEM] * len(arrays),
        out_specs=(VMEM,) * outs if outs > 1 else VMEM,
        cost_estimate=pl.CostEstimate(flops=flops, bytes_accessed=moved, transcendentals=0),
        name=name,
    )(*smem, *arrays)


def local(boundary, peps_row, sketch, charges, left_edge):
    sites = lax.axis_size("site")
    sectors = lax.axis_size("sector")
    position = lax.axis_index("site")
    block = lax.axis_index("sector")
    x, y = position // GROUP, lax.rem(position, GROUP)
    rows, width = left_edge.shape
    slab = rows // GROUP

    inside = [(i, i ^ 1) for i in range(sectors)]
    across = [(i, (i - 1) % sectors if i % 2 == 0 else (i + 1) % sectors) for i in range(sectors)]
    ring = lambda by: [(i, i - i % GROUP + (i + by) % GROUP) for i in range(sites)]
    hop = [(i, (i + GROUP) % sites) for i in range(sites)]

    odd = lax.rem(block, 2)
    sign = jnp.full((1,), 1, jnp.int32) - 2 * odd
    edge = jnp.logical_or(block == 0, block == sectors - 1).astype(jnp.int32).reshape(1)

    top, bottom = transfer(boundary, peps_row, sketch, charges, sign)
    up_top = lax.ppermute(top, "site", ring(-1))
    down_bottom = lax.ppermute(bottom, "site", ring(1))
    up_bottom = lax.ppermute(bottom, "site", ring(-1))
    down_top = lax.ppermute(top, "site", ring(1))
    far_top = lax.ppermute(up_top, "site", ring(-1))
    far_bottom = lax.ppermute(down_bottom, "site", ring(1))
    pieces = (top, bottom, up_top, up_bottom, far_top, far_bottom, down_top, down_bottom)

    state = lax.dynamic_slice_in_dim(left_edge, y * slab, slab, 0).astype(jnp.float32)
    transfers = [
        prepare(lax.rem(GROUP + j - y, GROUP).reshape(1), pieces) for j in range(GROUP)
    ]

    kept = [None] * GROUP
    for phase in range(sites // GROUP):
        out_a, out_b = call(away_kernel, 2, (), (state, *transfers[0]), 2, "away")
        for j in range(GROUP):
            from_b = lax.ppermute(out_b, "sector", across)
            from_a = lax.ppermute(out_a, "sector", inside)
            stay = call(stay_kernel, 1, (), (state, *transfers[j]), 1, "stay")
            if j < GROUP - 1:
                state, out_a, out_b = call(
                    sum_away_kernel, 3, (edge,), (stay, from_a, from_b, *transfers[j + 1]), 2, "sum_away"
                )
            else:
                state = call(sum_kernel, 1, (edge,), (stay, from_a, from_b), 0, "sum")
            kept[j] = state if phase == 0 else jnp.where(x == phase, state, kept[j])
        if phase < sites // GROUP - 1:
            state = lax.ppermute(state, "site", hop)

    stacked = jnp.stack(kept)
    result = jnp.zeros((1, rows, width), jnp.float32)
    for by in range(GROUP):
        out = lax.dynamic_index_in_dim(stacked, lax.rem(y + by, GROUP), 0, keepdims=True)
        if by:
            out = lax.ppermute(out, "site", ring(by))
        at = lax.rem(GROUP + y - by, GROUP) * slab
        result = lax.dynamic_update_slice(result, out, (0, at, 0))
    return result


def solution(mesh):
    in_specs = (
        P("site", "sector", None, None),
        P("site", None, None),
        P("site", "sector", None, None),
        P("site", None),
        P(None, "sector"),
    )
    out_specs = P("site", None, "sector")
    return jax.shard_map(local, mesh=mesh, in_specs=in_specs, out_specs=out_specs, check_vma=False)
```

time: 474 us -> 227 us (0.48)
  the two profiles are of different devices: /device:TPU:126 before, /device:TPU:1 now
where the time goes in v1:
time: 227 us; the launch traced here: 226 us
  Pallas kernels  87.5 us (39%)
  waiting for transfers between devices  78.2 us (34%)
  starting transfers between devices  38.6 us (17%)
  local copies, waits for them, and re-layouts  19.7 us (9%)
    pallas_call x36, Pallas kernels, call(): pl.pallas_call(kernel, out_shape=(shape,) * outs if outs > 1 else shape,...  75.5 us
    ppermute x16, waiting for transfers between devices, local(): from_b = lax.ppermute(out_b, 'sector', across)  37.7 us
    ppermute x16, starting transfers between devices, local(): from_a = lax.ppermute(out_a, 'sector', inside)  23.1 us
    unnamed x119, local copies, waits for them, and re-layouts  18.9 us
    ppermute x3, waiting for transfers between devices, local(): state = lax.ppermute(state, 'site', hop)  14.5 us
    pallas_call x4, Pallas kernels, prepare(): pl.pallas_call(prepare_kernel, out_shape=(out, out), in_specs=[SMEM] + [A...  8.37 us
    ppermute x3, waiting for transfers between devices, local(): out = lax.ppermute(out, 'site', ring(by))  5.92 us
    ppermute x1, waiting for transfers between devices, local(): far_top = lax.ppermute(up_top, 'site', ring(-1))  5.33 us
  transfers between devices with their start and end apart: 44, of which 24 were waited for; matrix products, arithmetic and copies ran while one was open for 1% of the time, Pallas kernels for 17%

profile of v1, /device:TPU:1, one launch (start us, length us, event | category | flops | bytes accessed | tf_op | source)
XLA Modules:
  0.0 226.2 jit_solution(1941582846582614518)
XLA Ops:
  4.8 3.7 %transfer.1 = (f32[384,256]{1,0:T(8,128)S(1)}, f32[384,256]{1,0:T(8,128)S(1)}) custom-call(s32[8]{0:T(128)S(1)} %bitcast.21, s32[1]{0:T(128)} %bitcast.3.sign_ref, bf16[32,8]{1,0:T(8,128)(2,1)S(1)} %bitcast.20, bf16[8192,256]{1,0:T(8,128)(2,1)S(1)} %bitcast.18, bf16[2048,256]{1,0:T(8,128)(2,1)S(1)} %bitcast.19), custom_call_target="tpu_custom_call" | custom-call | tf_op jit(solution)/shard_map/transfer/pallas_call | solution.py:81
  8.6 3.6 %collective-permute-start = (f32[384,256]{1,0:T(8,128)S(1)}, f32[384,256]{1,0:T(8,128)S(1)}, u32[]{:S(2)}, u32[]{:S(2)}) collective-permute-start(f32[384,256]{1,0:T(8,128)S(1)} %get-tuple-element.59.refs_0_), channel_id=1, source_target_pairs={{0,48},{16,0},{32,16},{48,32},{64,112},{80,64},{96,80},{112,96},{1... | collective-permute-start | bytes 1179656 | tf_op jit(solution)/shard_map/ppermute | solution.py:211
  14.9 5.1 %collective-permute-done.refs_2_ = f32[384,256]{1,0:T(8,128)S(1)} collective-permute-done((f32[384,256]{1,0:T(8,128)S(1)}, f32[384,256]{1,0:T(8,128)S(1)}, u32[]{:S(2)}, u32[]{:S(2)}) %collective-permute-start) | collective-permute-done | bytes 393248 | tf_op jit(solution)/shard_map/ppermute | solution.py:211
  20.0 3.4 %collective-permute-start.2 = (f32[384,256]{1,0:T(8,128)S(1)}, f32[384,256]{1,0:T(8,128)S(1)}, u32[]{:S(2)}, u32[]{:S(2)}) collective-permute-start(f32[384,256]{1,0:T(8,128)S(1)} %collective-permute-done.refs_2_), channel_id=1, source_target_pairs={{0,48},{16,0},{32,16},{48,32},{64,112},{80,64},{96,80},{112,96},{1... | collective-permute-start | bytes 1179656 | tf_op jit(solution)/shard_map/ppermute | solution.py:215
  25.0 3.4 %collective-permute-done.1.refs_3_ = f32[384,256]{1,0:T(8,128)S(1)} collective-permute-done((f32[384,256]{1,0:T(8,128)S(1)}, f32[384,256]{1,0:T(8,128)S(1)}, u32[]{:S(2)}, u32[]{:S(2)}) %collective-permute-start.1) | collective-permute-done | bytes 393248 | tf_op jit(solution)/shard_map/ppermute | solution.py:213
  28.4 3.1 %collective-permute-done.5.refs_6_ = f32[384,256]{1,0:T(8,128)S(1)} collective-permute-done((f32[384,256]{1,0:T(8,128)S(1)}, f32[384,256]{1,0:T(8,128)S(1)}, u32[]{:S(2)}, u32[]{:S(2)}) %collective-permute-start.5) | collective-permute-done | bytes 393248 | tf_op jit(solution)/shard_map/ppermute | solution.py:214
  31.5 5.3 %collective-permute-done.2.refs_4_ = f32[384,256]{1,0:T(8,128)S(1)} collective-permute-done((f32[384,256]{1,0:T(8,128)S(1)}, f32[384,256]{1,0:T(8,128)S(1)}, u32[]{:S(2)}, u32[]{:S(2)}) %collective-permute-start.2) | collective-permute-done | bytes 393248 | tf_op jit(solution)/shard_map/ppermute | solution.py:215
  36.9 3.1 %collective-permute-done.4.refs_5_ = f32[384,256]{1,0:T(8,128)S(1)} collective-permute-done((f32[384,256]{1,0:T(8,128)S(1)}, f32[384,256]{1,0:T(8,128)S(1)}, u32[]{:S(2)}, u32[]{:S(2)}) %collective-permute-start.4) | collective-permute-done | bytes 393248 | tf_op jit(solution)/shard_map/ppermute | solution.py:216
  55.5 4.4 %collective-permute-start.8 = (f32[128,256]{1,0:T(8,128)}, f32[128,256]{1,0:T(8,128)S(1)}, u32[]{:S(2)}, u32[]{:S(2)}) collective-permute-start(f32[128,256]{1,0:T(8,128)} %get-tuple-element.68), channel_id=1, source_target_pairs={{0,1},{1,0},{2,3},{3,2},{4,5},{5,4},{6,7},{7,6},{8,9},{9,8},{10,11... | collective-permute-start | bytes 393224 | tf_op jit(solution)/shard_map/ppermute | solution.py:229
  85.9 4.0 %collective-permute-done.14.state_ref = f32[128,256]{1,0:T(8,128)S(1)} collective-permute-done((f32[128,256]{1,0:T(8,128)}, f32[128,256]{1,0:T(8,128)S(1)}, u32[]{:S(2)}, u32[]{:S(2)}) %collective-permute-start.14) | collective-permute-done | bytes 131104 | tf_op jit(solution)/shard_map/ppermute | solution.py:239
  96.8 2.8 %collective-permute-done.16.from_b = f32[128,256]{1,0:T(8,128)S(1)} collective-permute-done((f32[128,256]{1,0:T(8,128)}, f32[128,256]{1,0:T(8,128)S(1)}, u32[]{:S(2)}, u32[]{:S(2)}) %collective-permute-start.16) | collective-permute-done | bytes 131104 | tf_op jit(solution)/shard_map/ppermute | solution.py:228
  105.6 2.8 %collective-permute-done.18.from_b = f32[128,256]{1,0:T(8,128)S(1)} collective-permute-done((f32[128,256]{1,0:T(8,128)}, f32[128,256]{1,0:T(8,128)S(1)}, u32[]{:S(2)}, u32[]{:S(2)}) %collective-permute-start.18) | collective-permute-done | bytes 131104 | tf_op jit(solution)/shard_map/ppermute | solution.py:228
  114.3 2.8 %collective-permute-done.20.from_b = f32[128,256]{1,0:T(8,128)S(1)} collective-permute-done((f32[128,256]{1,0:T(8,128)}, f32[128,256]{1,0:T(8,128)S(1)}, u32[]{:S(2)}, u32[]{:S(2)}) %collective-permute-start.20) | collective-permute-done | bytes 131104 | tf_op jit(solution)/shard_map/ppermute | solution.py:228
  123.1 2.8 %collective-permute-done.22.from_b = f32[128,256]{1,0:T(8,128)S(1)} collective-permute-done((f32[128,256]{1,0:T(8,128)}, f32[128,256]{1,0:T(8,128)S(1)}, u32[]{:S(2)}, u32[]{:S(2)}) %collective-permute-start.22) | collective-permute-done | bytes 131104 | tf_op jit(solution)/shard_map/ppermute | solution.py:228
  128.2 5.2 %collective-permute-done.23.state_ref = f32[128,256]{1,0:T(8,128)S(1)} collective-permute-done((f32[128,256]{1,0:T(8,128)}, f32[128,256]{1,0:T(8,128)S(1)}, u32[]{:S(2)}, u32[]{:S(2)}) %collective-permute-start.23) | collective-permute-done | bytes 131104 | tf_op jit(solution)/shard_map/ppermute | solution.py:239
  140.5 2.8 %collective-permute-done.25.from_b = f32[128,256]{1,0:T(8,128)S(1)} collective-permute-done((f32[128,256]{1,0:T(8,128)}, f32[128,256]{1,0:T(8,128)S(1)}, u32[]{:S(2)}, u32[]{:S(2)}) %collective-permute-start.25) | collective-permute-done | bytes 131104 | tf_op jit(solution)/shard_map/ppermute | solution.py:228
  149.2 2.8 %collective-permute-done.27.from_b = f32[128,256]{1,0:T(8,128)S(1)} collective-permute-done((f32[128,256]{1,0:T(8,128)}, f32[128,256]{1,0:T(8,128)S(1)}, u32[]{:S(2)}, u32[]{:S(2)}) %collective-permute-start.27) | collective-permute-done | bytes 131104 | tf_op jit(solution)/shard_map/ppermute | solution.py:228
  158.0 2.8 %collective-permute-done.29.from_b = f32[128,256]{1,0:T(8,128)S(1)} collective-permute-done((f32[128,256]{1,0:T(8,128)}, f32[128,256]{1,0:T(8,128)S(1)}, u32[]{:S(2)}, u32[]{:S(2)}) %collective-permute-start.29) | collective-permute-done | bytes 131104 | tf_op jit(solution)/shard_map/ppermute | solution.py:228
  166.9 2.8 %collective-permute-done.31.from_b = f32[128,256]{1,0:T(8,128)S(1)} collective-permute-done((f32[128,256]{1,0:T(8,128)}, f32[128,256]{1,0:T(8,128)S(1)}, u32[]{:S(2)}, u32[]{:S(2)}) %collective-permute-start.31) | collective-permute-done | bytes 131104 | tf_op jit(solution)/shard_map/ppermute | solution.py:228
  172.1 5.2 %collective-permute-done.32.state_ref = f32[128,256]{1,0:T(8,128)S(1)} collective-permute-done((f32[128,256]{1,0:T(8,128)}, f32[128,256]{1,0:T(8,128)S(1)}, u32[]{:S(2)}, u32[]{:S(2)}) %collective-permute-start.32) | collective-permute-done | bytes 131104 | tf_op jit(solution)/shard_map/ppermute | solution.py:239
  184.3 2.8 %collective-permute-done.34.from_b = f32[128,256]{1,0:T(8,128)S(1)} collective-permute-done((f32[128,256]{1,0:T(8,128)}, f32[128,256]{1,0:T(8,128)S(1)}, u32[]{:S(2)}, u32[]{:S(2)}) %collective-permute-start.34) | collective-permute-done | bytes 131104 | tf_op jit(solution)/shard_map/ppermute | solution.py:228
  193.2 2.8 %collective-permute-done.36.from_b = f32[128,256]{1,0:T(8,128)S(1)} collective-permute-done((f32[128,256]{1,0:T(8,128)}, f32[128,256]{1,0:T(8,128)S(1)}, u32[]{:S(2)}, u32[]{:S(2)}) %collective-permute-start.36) | collective-permute-done | bytes 131104 | tf_op jit(solution)/shard_map/ppermute | solution.py:228
  210.7 2.8 %collective-permute-done.40.from_b = f32[128,256]{1,0:T(8,128)S(1)} collective-permute-done((f32[128,256]{1,0:T(8,128)}, f32[128,256]{1,0:T(8,128)S(1)}, u32[]{:S(2)}, u32[]{:S(2)}) %collective-permute-start.40) | collective-permute-done | bytes 131104 | tf_op jit(solution)/shard_map/ppermute | solution.py:228
  218.8 5.9 %collective-permute-done.41 = f32[1,128,256]{2,1,0:T(8,128)S(1)} collective-permute-done((f32[1,128,256]{2,1,0:T(8,128)S(1)}, f32[1,128,256]{2,1,0:T(8,128)S(1)}, u32[]{:S(2)}, u32[]{:S(2)}) %collective-permute-start.41) | collective-permute-done | bytes 131104 | tf_op jit(solution)/shard_map/ppermute | solution.py:246
  (235 shorter events, 139.2 us)
Async XLA Ops:
  8.6 11.4 %collective-permute-start = (f32[384,256]{1,0:T(8,128)S(1)}, f32[384,256]{1,0:T(8,128)S(1)}, u32[]{:S(2)}, u32[]{:S(2)}) collective-permute-start(f32[384,256]{1,0:T(8,128)S(1)} %get-tuple-element.59.refs_0_), channel_id=1, source_target_pairs={{0,48},{16,0},{32,16},{48,32},{64,112},{80,64},{96,80},{112,96},{1... | collective-permute-start | bytes 1179656 | tf_op jit(solution)/shard_map/ppermute | solution.py:211
  12.2 11.2 %collective-permute-start.3 = (f32[384,256]{1,0:T(8,128)S(1)}, f32[384,256]{1,0:T(8,128)S(1)}, u32[]{:S(2)}, u32[]{:S(2)}) collective-permute-start(f32[384,256]{1,0:T(8,128)S(1)} %get-tuple-element.60.refs_1_), channel_id=1, source_target_pairs={{0,16},{16,32},{32,48},{48,0},{64,80},{80,96},{96,112},{112,64},{1... | collective-permute-start | bytes 1179656 | tf_op jit(solution)/shard_map/ppermute | solution.py:212
  12.2 16.2 %collective-permute-start.1 = (f32[384,256]{1,0:T(8,128)S(1)}, f32[384,256]{1,0:T(8,128)S(1)}, u32[]{:S(2)}, u32[]{:S(2)}) collective-permute-start(f32[384,256]{1,0:T(8,128)S(1)} %get-tuple-element.60.refs_1_), channel_id=1, source_target_pairs={{0,48},{16,0},{32,16},{48,32},{64,112},{80,64},{96,80},{112,96},{1... | collective-permute-start | bytes 1179656 | tf_op jit(solution)/shard_map/ppermute | solution.py:213
  14.9 16.6 %collective-permute-start.5 = (f32[384,256]{1,0:T(8,128)S(1)}, f32[384,256]{1,0:T(8,128)S(1)}, u32[]{:S(2)}, u32[]{:S(2)}) collective-permute-start(f32[384,256]{1,0:T(8,128)S(1)} %get-tuple-element.59.refs_0_), channel_id=1, source_target_pairs={{0,16},{16,32},{32,48},{48,0},{64,80},{80,96},{96,112},{112,64},{1... | collective-permute-start | bytes 1179656 | tf_op jit(solution)/shard_map/ppermute | solution.py:214
  20.0 16.9 %collective-permute-start.2 = (f32[384,256]{1,0:T(8,128)S(1)}, f32[384,256]{1,0:T(8,128)S(1)}, u32[]{:S(2)}, u32[]{:S(2)}) collective-permute-start(f32[384,256]{1,0:T(8,128)S(1)} %collective-permute-done.refs_2_), channel_id=1, source_target_pairs={{0,48},{16,0},{32,16},{48,32},{64,112},{80,64},{96,80},{112,96},{1... | collective-permute-start | bytes 1179656 | tf_op jit(solution)/shard_map/ppermute | solution.py:215
  23.4 16.5 %collective-permute-start.4 = (f32[384,256]{1,0:T(8,128)S(1)}, f32[384,256]{1,0:T(8,128)S(1)}, u32[]{:S(2)}, u32[]{:S(2)}) collective-permute-start(f32[384,256]{1,0:T(8,128)S(1)} %collective-permute-done.3.refs_7_), channel_id=1, source_target_pairs={{0,16},{16,32},{32,48},{48,0},{64,80},{80,96},{96,112},{112,64},{1... | collective-permute-start | bytes 1179656 | tf_op jit(solution)/shard_map/ppermute | solution.py:216
  44.9 7.6 %collective-permute-start.6 = (f32[128,256]{1,0:T(8,128)}, f32[128,256]{1,0:T(8,128)S(1)}, u32[]{:S(2)}, u32[]{:S(2)}) collective-permute-start(f32[128,256]{1,0:T(8,128)} %get-tuple-element.63), channel_id=1, source_target_pairs={{0,1},{1,0},{2,3},{3,2},{4,5},{5,4},{6,7},{7,6},{8,9},{9,8},{10,11... | collective-permute-start | bytes 393224 | tf_op jit(solution)/shard_map/ppermute | solution.py:229
  46.8 5.7 %collective-permute-start.7 = (f32[128,256]{1,0:T(8,128)}, f32[128,256]{1,0:T(8,128)S(1)}, u32[]{:S(2)}, u32[]{:S(2)}) collective-permute-start(f32[128,256]{1,0:T(8,128)} %get-tuple-element.64), channel_id=1, source_target_pairs={{0,15},{1,2},{2,1},{3,4},{4,3},{5,6},{6,5},{7,8},{8,7},{9,10},{10,... | collective-permute-start | bytes 393224 | tf_op jit(solution)/shard_map/ppermute | solution.py:228
  55.5 8.6 %collective-permute-start.8 = (f32[128,256]{1,0:T(8,128)}, f32[128,256]{1,0:T(8,128)S(1)}, u32[]{:S(2)}, u32[]{:S(2)}) collective-permute-start(f32[128,256]{1,0:T(8,128)} %get-tuple-element.68), channel_id=1, source_target_pairs={{0,1},{1,0},{2,3},{3,2},{4,5},{5,4},{6,7},{7,6},{8,9},{9,8},{10,11... | collective-permute-start | bytes 393224 | tf_op jit(solution)/shard_map/ppermute | solution.py:229
  59.9 4.9 %collective-permute-start.9 = (f32[128,256]{1,0:T(8,128)}, f32[128,256]{1,0:T(8,128)S(1)}, u32[]{:S(2)}, u32[]{:S(2)}) collective-permute-start(f32[128,256]{1,0:T(8,128)} %get-tuple-element.69), channel_id=1, source_target_pairs={{0,15},{1,2},{2,1},{3,4},{4,3},{5,6},{6,5},{7,8},{8,7},{9,10},{10,... | collective-permute-start | bytes 393224 | tf_op jit(solution)/shard_map/ppermute | solution.py:228
  67.7 5.2 %collective-permute-start.10 = (f32[128,256]{1,0:T(8,128)}, f32[128,256]{1,0:T(8,128)S(1)}, u32[]{:S(2)}, u32[]{:S(2)}) collective-permute-start(f32[128,256]{1,0:T(8,128)} %get-tuple-element.73), channel_id=1, source_target_pairs={{0,1},{1,0},{2,3},{3,2},{4,5},{5,4},{6,7},{7,6},{8,9},{9,8},{10,11... | collective-permute-start | bytes 393224 | tf_op jit(solution)/shard_map/ppermute | solution.py:229
  68.7 4.9 %collective-permute-start.11 = (f32[128,256]{1,0:T(8,128)}, f32[128,256]{1,0:T(8,128)S(1)}, u32[]{:S(2)}, u32[]{:S(2)}) collective-permute-start(f32[128,256]{1,0:T(8,128)} %get-tuple-element.74), channel_id=1, source_target_pairs={{0,15},{1,2},{2,1},{3,4},{4,3},{5,6},{6,5},{7,8},{8,7},{9,10},{10,... | collective-permute-start | bytes 393224 | tf_op jit(solution)/shard_map/ppermute | solution.py:228
  77.4 4.9 %collective-permute-start.13 = (f32[128,256]{1,0:T(8,128)}, f32[128,256]{1,0:T(8,128)S(1)}, u32[]{:S(2)}, u32[]{:S(2)}) collective-permute-start(f32[128,256]{1,0:T(8,128)} %get-tuple-element.79), channel_id=1, source_target_pairs={{0,15},{1,2},{2,1},{3,4},{4,3},{5,6},{6,5},{7,8},{8,7},{9,10},{10,... | collective-permute-start | bytes 393224 | tf_op jit(solution)/shard_map/ppermute | solution.py:228
  84.6 5.2 %collective-permute-start.14 = (f32[128,256]{1,0:T(8,128)}, f32[128,256]{1,0:T(8,128)S(1)}, u32[]{:S(2)}, u32[]{:S(2)}) collective-permute-start(f32[128,256]{1,0:T(8,128)} %sum.4), channel_id=1, source_target_pairs={{0,64},{16,80},{32,96},{48,112},{64,128},{80,144},{96,160},{112,17... | collective-permute-start | bytes 393224 | tf_op jit(solution)/shard_map/ppermute | solution.py:239
  94.8 4.9 %collective-permute-start.16 = (f32[128,256]{1,0:T(8,128)}, f32[128,256]{1,0:T(8,128)S(1)}, u32[]{:S(2)}, u32[]{:S(2)}) collective-permute-start(f32[128,256]{1,0:T(8,128)} %get-tuple-element.81), channel_id=1, source_target_pairs={{0,15},{1,2},{2,1},{3,4},{4,3},{5,6},{6,5},{7,8},{8,7},{9,10},{10,... | collective-permute-start | bytes 393224 | tf_op jit(solution)/shard_map/ppermute | solution.py:228
  103.5 4.9 %collective-permute-start.18 = (f32[128,256]{1,0:T(8,128)}, f32[128,256]{1,0:T(8,128)S(1)}, u32[]{:S(2)}, u32[]{:S(2)}) collective-permute-start(f32[128,256]{1,0:T(8,128)} %get-tuple-element.84), channel_id=1, source_target_pairs={{0,15},{1,2},{2,1},{3,4},{4,3},{5,6},{6,5},{7,8},{8,7},{9,10},{10,... | collective-permute-start | bytes 393224 | tf_op jit(solution)/shard_map/ppermute | solution.py:228
  112.3 4.9 %collective-permute-start.20 = (f32[128,256]{1,0:T(8,128)}, f32[128,256]{1,0:T(8,128)S(1)}, u32[]{:S(2)}, u32[]{:S(2)}) collective-permute-start(f32[128,256]{1,0:T(8,128)} %get-tuple-element.87), channel_id=1, source_target_pairs={{0,15},{1,2},{2,1},{3,4},{4,3},{5,6},{6,5},{7,8},{8,7},{9,10},{10,... | collective-permute-start | bytes 393224 | tf_op jit(solution)/shard_map/ppermute | solution.py:228
  121.0 4.9 %collective-permute-start.22 = (f32[128,256]{1,0:T(8,128)}, f32[128,256]{1,0:T(8,128)S(1)}, u32[]{:S(2)}, u32[]{:S(2)}) collective-permute-start(f32[128,256]{1,0:T(8,128)} %get-tuple-element.90), channel_id=1, source_target_pairs={{0,15},{1,2},{2,1},{3,4},{4,3},{5,6},{6,5},{7,8},{8,7},{9,10},{10,... | collective-permute-start | bytes 393224 | tf_op jit(solution)/shard_map/ppermute | solution.py:228
  128.2 5.2 %collective-permute-start.23 = (f32[128,256]{1,0:T(8,128)}, f32[128,256]{1,0:T(8,128)S(1)}, u32[]{:S(2)}, u32[]{:S(2)}) collective-permute-start(f32[128,256]{1,0:T(8,128)} %sum.5), channel_id=1, source_target_pairs={{0,64},{16,80},{32,96},{48,112},{64,128},{80,144},{96,160},{112,17... | collective-permute-start | bytes 393224 | tf_op jit(solution)/shard_map/ppermute | solution.py:239
  164.8 4.9 %collective-permute-start.31 = (f32[128,256]{1,0:T(8,128)}, f32[128,256]{1,0:T(8,128)S(1)}, u32[]{:S(2)}, u32[]{:S(2)}) collective-permute-start(f32[128,256]{1,0:T(8,128)} %get-tuple-element.101), channel_id=1, source_target_pairs={{0,15},{1,2},{2,1},{3,4},{4,3},{5,6},{6,5},{7,8},{8,7},{9,10},{10,... | collective-permute-start | bytes 393224 | tf_op jit(solution)/shard_map/ppermute | solution.py:228
  172.0 5.2 %collective-permute-start.32 = (f32[128,256]{1,0:T(8,128)}, f32[128,256]{1,0:T(8,128)S(1)}, u32[]{:S(2)}, u32[]{:S(2)}) collective-permute-start(f32[128,256]{1,0:T(8,128)} %sum.6), channel_id=1, source_target_pairs={{0,64},{16,80},{32,96},{48,112},{64,128},{80,144},{96,160},{112,17... | collective-permute-start | bytes 393224 | tf_op jit(solution)/shard_map/ppermute | solution.py:239
  216.0 8.7 %collective-permute-start.41 = (f32[1,128,256]{2,1,0:T(8,128)S(1)}, f32[1,128,256]{2,1,0:T(8,128)S(1)}, u32[]{:S(2)}, u32[]{:S(2)}) collective-permute-start(f32[1,128,256]{2,1,0:T(8,128)S(1)} %get-tuple-element.115), channel_id=1, source_target_pairs={{0,16},{16,32},{32,48},{48,0},{64,80},{80,96},{96,112},{112,64},{1... | collective-permute-start | bytes 393224 | tf_op jit(solution)/shard_map/ppermute | solution.py:246
  216.1 8.6 %collective-permute-start.42 = (f32[1,128,256]{2,1,0:T(8,128)S(1)}, f32[1,128,256]{2,1,0:T(8,128)S(1)}, u32[]{:S(2)}, u32[]{:S(2)}) collective-permute-start(f32[1,128,256]{2,1,0:T(8,128)S(1)} %get-tuple-element.114), channel_id=1, source_target_pairs={{0,32},{16,48},{32,0},{48,16},{64,96},{80,112},{96,64},{112,80},{1... | collective-permute-start | bytes 393224 | tf_op jit(solution)/shard_map/ppermute | solution.py:246
  217.4 7.3 %collective-permute-start.43 = (f32[1,128,256]{2,1,0:T(8,128)S(1)}, f32[1,128,256]{2,1,0:T(8,128)S(1)}, u32[]{:S(2)}, u32[]{:S(2)}) collective-permute-start(f32[1,128,256]{2,1,0:T(8,128)S(1)} %get-tuple-element.113), channel_id=1, source_target_pairs={{0,48},{16,0},{32,16},{48,32},{64,112},{80,64},{96,80},{112,96},{1... | collective-permute-start | bytes 393224 | tf_op jit(solution)/shard_map/ppermute | solution.py:246
  (79 other events, 638.7 us)

commit v2 on v0

v2 whole, which is shorter than its diff:
```python
import functools

import jax
import jax.numpy as jnp
from jax import lax
from jax.experimental import pallas as pl
from jax.experimental.pallas import tpu as pltpu
from jax.sharding import PartitionSpec as P

GROUP = 4
CHARGES = 3
LANES = 128
SMALL = 12 * 2**20
LARGE = 56 * 2**20


def dot(a, b):
    return jnp.dot(a, b, preferred_element_type=jnp.float32)


def split(x):
    high = x.astype(jnp.bfloat16)
    return high, (x - high.astype(jnp.float32)).astype(jnp.bfloat16)


def transfer_kernel(x_ref, y_ref, sign_ref, inner_ref, charge_ref, peps_ref, boundary_ref, sketch_ref, top_ref, bottom_ref,
                    boundary, sketch, spread, absorbed, wide, total, sems):
    width = total.shape[1]
    bonds, phys = peps_ref.shape
    per = width // phys
    parts = sems.shape[0] - 1
    span = boundary.shape[0] // parts
    chunks = span // width

    def fetch(part):
        rows = pl.ds(part * span, span)
        return pltpu.make_async_copy(boundary_ref.at[rows], boundary.at[rows], sems.at[part])

    fetch_sketch = pltpu.make_async_copy(sketch_ref, sketch, sems.at[parts])
    for part in range(parts):
        fetch(part).start()
    fetch_sketch.start()

    row = lax.broadcasted_iota(jnp.int32, (phys, width), 0)
    col = lax.broadcasted_iota(jnp.int32, (phys, width), 1)
    tiled = jnp.where(lax.rem(col, phys) == row, 1.0, 0.0).astype(jnp.bfloat16)
    repeated = lax.dot_general(
        peps_ref[...], tiled, (((1,), (0,)), ((), ())), preferred_element_type=jnp.float32
    )
    rows = bonds * per
    pick_row = lax.broadcasted_iota(jnp.int32, (rows, bonds), 0)
    pick_col = lax.broadcasted_iota(jnp.int32, (rows, bonds), 1)
    pick = jnp.where(lax.div(pick_row, per) == pick_col, 1.0, 0.0).astype(jnp.bfloat16)
    spread_rows = dot(pick, repeated.astype(jnp.bfloat16))
    out_row = lax.broadcasted_iota(jnp.int32, (rows, width), 0)
    out_col = lax.broadcasted_iota(jnp.int32, (rows, width), 1)
    keep = lax.rem(out_row, per) == lax.div(out_col, phys)
    spread[...] = jnp.where(keep, spread_rows, 0.0).astype(jnp.bfloat16)

    for part in range(parts):
        fetch(part).wait()
        for chunk in range(part * chunks, (part + 1) * chunks):
            piece = dot(spread[...], boundary[chunk * width:(chunk + 1) * width, :])
            for bond in range(bonds):
                absorbed[bond, chunk * per:(chunk + 1) * per, :] = piece[bond * per:(bond + 1) * per]

    fetch_sketch.wait()
    for lane in range(width // LANES):
        wide[lane] = sketch[:, lane * LANES:(lane + 1) * LANES].astype(jnp.float32)
    total[...] = jnp.zeros_like(total)
    for bond in range(bonds):
        high, low = split(absorbed[bond])
        lanes = [wide[lane, pl.ds(bond, width, stride=bonds), :] for lane in range(width // LANES)]
        part = jnp.concatenate(lanes, axis=1).astype(jnp.bfloat16)
        both = dot(jnp.concatenate([high, low], axis=0), part)
        slot = 1 + charge_ref[bond] * sign_ref[0]
        where = pl.ds(pl.multiple_of(slot * width, width), width)
        total[where, :] += both[:width] + both[width:]
    half = total.shape[0] // 2
    top_ref[...] = total[:half]
    bottom_ref[...] = total[half:]


VMEM = pl.BlockSpec(memory_space=pltpu.VMEM)
SMEM = pl.BlockSpec(memory_space=pltpu.SMEM)
ANY = pl.BlockSpec(memory_space=pl.ANY)


def transfer(info, boundary, peps_row, sketch, charges):
    width = boundary.shape[3]
    phys, bonds = peps_row.shape[1:]
    parts = 8
    half = jax.ShapeDtypeStruct((CHARGES * width // 2, width), jnp.float32)
    return pl.pallas_call(
        transfer_kernel,
        out_shape=(half, half),
        in_specs=[SMEM] * 5 + [VMEM, ANY, ANY],
        out_specs=(VMEM, VMEM),
        scratch_shapes=[
            pltpu.VMEM((width * phys, width), jnp.bfloat16),
            pltpu.VMEM((width * bonds, width), jnp.bfloat16),
            pltpu.VMEM((bonds * width // phys, width), jnp.bfloat16),
            pltpu.VMEM((bonds, width, width), jnp.float32),
            pltpu.VMEM((width // LANES, width * bonds, LANES), jnp.float32),
            pltpu.VMEM((CHARGES * width, width), jnp.float32),
            pltpu.SemaphoreType.DMA((parts + 1,)),
        ],
        compiler_params=pltpu.CompilerParams(vmem_limit_bytes=LARGE),
        name="transfer",
    )(*info, charges[0], peps_row[0].T, boundary.reshape(width * phys, width), sketch.reshape(width * bonds, width))


def times(state, high, low):
    rows = state.shape[0]
    state_high, state_low = split(state)
    first = dot(jnp.concatenate([state_high, state_low], axis=0), high)
    return first[:rows] + first[rows:] + dot(state_high, low)


def call(kernel, outs, scalars, arrays, tiles=0, aliases={}, name=None):
    moved = sum(a.size * a.dtype.itemsize for a in arrays)
    rows, width = 128, 256
    shapes = tuple(jax.ShapeDtypeStruct(*out) for out in outs)
    return pl.pallas_call(
        kernel,
        out_shape=shapes,
        in_specs=[SMEM] * len(scalars) + [VMEM] * len(arrays),
        out_specs=(VMEM,) * len(outs),
        input_output_aliases=aliases,
        cost_estimate=pl.CostEstimate(
            flops=6 * tiles * rows * width * width, bytes_accessed=moved, transcendentals=0
        ),
        compiler_params=pltpu.CompilerParams(vmem_limit_bytes=SMALL),
        name=name,
    )(*scalars, *arrays)


def place_kernel(k, y_ref, top_ref, bottom_ref, *refs):
    high_ref, low_ref = refs[-2:]
    half = top_ref.shape[0]
    at = lax.rem(y_ref[0] + k, GROUP) * (2 * half)
    for ref, offset in ((top_ref, 0), (bottom_ref, half)):
        where = pl.ds(pl.multiple_of(at + offset, half), half)
        high, low = split(ref[...])
        high_ref[where, :] = high
        low_ref[where, :] = low


def place(info, k, top, bottom, placed):
    half, width = top.shape
    out = ((GROUP * 2 * half, width), jnp.bfloat16)
    aliases = {3: 0, 4: 1} if placed else {}
    return call(
        functools.partial(place_kernel, k), (out, out), (info[Y],), (top, bottom, *placed), 0, aliases, "place"
    )


def columns(site, slot, width):
    start = (site * CHARGES + slot) * width
    return slice(start, start + width)


def away_of(site, state, high_ref, low_ref, out_a, out_b):
    width = state.shape[1]
    for slot, out in ((0, out_b), (2, out_a)):
        where = columns(site, slot, width)
        out[...] = times(state, high_ref[where], low_ref[where])


def edge_kernel(y_ref, edge_ref, high_ref, low_ref, state_ref, out_a, out_b):
    slab = state_ref.shape[0]
    at = pl.multiple_of(y_ref[0] * slab, slab)
    state = edge_ref[pl.ds(at, slab), :].astype(jnp.float32)
    state_ref[...] = state
    away_of(0, state, high_ref, low_ref, out_a, out_b)


def away_kernel(state_ref, high_ref, low_ref, out_a, out_b):
    away_of(0, state_ref[...], high_ref, low_ref, out_a, out_b)


def summed(inner_ref, stay_ref, from_a, from_b):
    return stay_ref[...] + from_a[...] + jnp.where(inner_ref[0] == 1, from_b[...], 0.0)


def sum_away_kernel(site, inner_ref, stay_ref, from_a, from_b, high_ref, low_ref, state_ref, out_a, out_b):
    state = summed(inner_ref, stay_ref, from_a, from_b)
    state_ref[...] = state
    away_of(site, state, high_ref, low_ref, out_a, out_b)


def keep_at(phase, site, x_ref, state, kept_ref):
    @pl.when(x_ref[0] == phase)
    def _():
        kept_ref[site] = state


def stay_kernel(phase, site, x_ref, state_ref, high_ref, low_ref, *refs):
    where = columns(site, 1, state_ref.shape[1])
    state = state_ref[...]
    if site:
        keep_at(phase, site - 1, x_ref, state, refs[-1])
        out_ref = refs[-2]
    else:
        out_ref = refs[-1]
    out_ref[...] = times(state, high_ref[where], low_ref[where])


def sum_kernel(phase, x_ref, inner_ref, stay_ref, from_a, from_b, old_ref, state_ref, kept_ref):
    state = summed(inner_ref, stay_ref, from_a, from_b)
    state_ref[...] = state
    keep_at(phase, GROUP - 1, x_ref, state, kept_ref)


def pick_kernel(y_ref, kept_ref, *outs):
    for by, out in enumerate(outs):
        out[...] = kept_ref[lax.rem(y_ref[0] + by + 1, GROUP)]


def lay_kernel(y_ref, kept_ref, *refs):
    out_ref = refs[-1]
    slab = kept_ref.shape[1]
    for by in range(GROUP):
        source = lax.rem(y_ref[0] + GROUP - by, GROUP)
        where = pl.ds(pl.multiple_of(source * slab, slab), slab)
        out_ref[0, where, :] = refs[by - 1][...] if by else kept_ref[y_ref[0]]


X, Y, SIGN, INNER = range(4)


def local(boundary, peps_row, sketch, charges, left_edge):
    sites = lax.axis_size("site")
    sectors = lax.axis_size("sector")
    position = lax.axis_index("site")
    block = lax.axis_index("sector")
    rows, width = left_edge.shape
    slab = rows // GROUP
    state_shape = ((slab, width), jnp.float32)
    kept_shape = ((GROUP, slab, width), jnp.float32)

    inside = [(i, i ^ 1) for i in range(sectors)]
    across = [(i, (i - 1) % sectors if i % 2 == 0 else (i + 1) % sectors) for i in range(sectors)]
    ring = lambda by: [(i, i - i % GROUP + (i + by) % GROUP) for i in range(sites)]
    hop = [(i, (i + GROUP) % sites) for i in range(sites)]

    inner = jnp.logical_and(block > 0, block < sectors - 1).astype(jnp.int32)
    info = [lax.div(position, GROUP), lax.rem(position, GROUP), 1 - 2 * lax.rem(block, 2), inner]
    info = lax.optimization_barrier([scalar.astype(jnp.int32).reshape(1) for scalar in info])

    top, bottom = transfer(info, boundary, peps_row, sketch, charges)
    up_top = lax.ppermute(top, "site", ring(-1))
    down_bottom = lax.ppermute(bottom, "site", ring(1))
    up_bottom = lax.ppermute(bottom, "site", ring(-1))
    down_top = lax.ppermute(top, "site", ring(1))
    far_top = lax.ppermute(up_top, "site", ring(-1))
    far_bottom = lax.ppermute(down_bottom, "site", ring(1))
    placed = place(info, 0, top, bottom, ())
    placed = place(info, 1, up_top, up_bottom, placed)
    placed = place(info, 3, down_top, down_bottom, placed)
    placed = place(info, 2, far_top, far_bottom, placed)

    state, out_a, out_b = call(
        edge_kernel, (state_shape,) * 3, (info[Y],), (left_edge, *placed), 2, name="away"
    )
    kept = None
    for phase in range(sites // GROUP):
        if phase:
            state = lax.ppermute(state, "site", hop)
            out_a, out_b = call(away_kernel, (state_shape,) * 2, (), (state, *placed), 2, name="away")
        for site in range(GROUP):
            from_b = lax.ppermute(out_b, "sector", across)
            from_a = lax.ppermute(out_a, "sector", inside)
            kernel = functools.partial(stay_kernel, phase, site)
            arrays = (state, *placed)
            if not site:
                stay, = call(kernel, (state_shape,), (info[X],), arrays, 1, name="stay")
            elif kept is None:
                stay, kept = call(kernel, (state_shape, kept_shape), (info[X],), arrays, 1, name="stay")
            else:
                stay, kept = call(kernel, (state_shape, kept_shape), (info[X],), (*arrays, kept), 1, {4: 1}, "stay")
            if site < GROUP - 1:
                kernel = functools.partial(sum_away_kernel, site + 1)
                arrays = (stay, from_a, from_b, *placed)
                state, out_a, out_b = call(kernel, (state_shape,) * 3, (info[INNER],), arrays, 2, name="sum_away")
            else:
                kernel = functools.partial(sum_kernel, phase)
                arrays = (stay, from_a, from_b, kept)
                scalars = (info[X], info[INNER])
                state, kept = call(kernel, (state_shape, kept_shape), scalars, arrays, 0, {5: 1}, "sum")

    sent = call(pick_kernel, (state_shape,) * (GROUP - 1), (info[Y],), (kept,), name="pick")
    came = [lax.ppermute(out, "site", ring(by + 1)) for by, out in enumerate(sent)]
    result, = call(lay_kernel, (((1, rows, width), jnp.float32),), (info[Y],), (kept, *came), name="lay")
    return result


def solution(mesh):
    in_specs = (
        P("site", "sector", None, None),
        P("site", None, None),
        P("site", "sector", None, None),
        P("site", None),
        P(None, "sector"),
    )
    out_specs = P("site", None, "sector")
    return jax.shard_map(local, mesh=mesh, in_specs=in_specs, out_specs=out_specs, check_vma=False)
```

time: 474 us -> 169 us (0.36)
  the two profiles are of different devices: /device:TPU:126 before, /device:TPU:1 now
where the time goes in v2:
time: 169 us; the launch traced here: 168 us
  waiting for transfers between devices  109 us (64%)
  starting transfers between devices  41.1 us (24%)
  Pallas kernels  15.5 us (9%)
  local copies, waits for them, and re-layouts  2.8 us (2%)
    ppermute x16, waiting for transfers between devices, local(): from_b = lax.ppermute(out_b, 'sector', across)  58 us
    ppermute x16, starting transfers between devices, local(): from_a = lax.ppermute(out_a, 'sector', inside)  25.6 us
    ppermute x3, waiting for transfers between devices, local(): state = lax.ppermute(state, 'site', hop)  13.9 us
    ppermute x16, waiting for transfers between devices, local(): from_a = lax.ppermute(out_a, 'sector', inside)  11.2 us
    pallas_call x42, Pallas kernels, call(): pl.pallas_call(kernel, out_shape=shapes, in_specs=[SMEM] * len(scalars) +...  10 us
    ppermute x3, waiting for transfers between devices, local(): lax.ppermute(out, 'site', ring(by + 1))  5.9 us
    pallas_call x1, Pallas kernels, transfer(): pl.pallas_call(transfer_kernel, out_shape=(half, half), in_specs=[SMEM] *...  5.51 us
    ppermute x1, waiting for transfers between devices, local(): up_top = lax.ppermute(top, 'site', ring(-1))  5.41 us
  transfers between devices with their start and end apart: 44, of which 40 were waited for; matrix products, arithmetic and copies ran while one was open for 0% of the time, Pallas kernels for 2%

profile of v2, /device:TPU:1, one launch (start us, length us, event | category | flops | bytes accessed | tf_op | source)
XLA Modules:
  0.0 168.3 jit_solution(13340505445190928345)
XLA Ops:
  0.0 5.5 %transfer.1 = (f32[384,256]{1,0:T(8,128)}, f32[384,256]{1,0:T(8,128)}) custom-call(s32[1]{0:T(128)} %bitcast.x_ref, s32[1]{0:T(128)} %bitcast.1.y_ref, s32[1]{0:T(128)} %bitcast.2.sign_ref, s32[1]{0:T(128)} %bitcast.3.inner_ref, s32[8]{0:T(128)} %bitcast.13, bf16[8,32]{1,0:T(8,128)(2,1)} %bitcast.12, bf16[8192,256]{1,0:T(8,128)(2,1)} %bitcast.10, ...), custom_call_target="tpu_custom_call" | custom-call | tf_op jit(solution)/shard_map/transfer/pallas_call | solution.py:94
  5.5 3.6 %collective-permute-start = (f32[384,256]{1,0:T(8,128)}, f32[384,256]{1,0:T(8,128)S(1)}, u32[]{:S(2)}, u32[]{:S(2)}) collective-permute-start(f32[384,256]{1,0:T(8,128)} %get-tuple-element.102.top_ref), channel_id=1, source_target_pairs={{0,48},{16,0},{32,16},{48,32},{64,112},{80,64},{96,80},{112,96},{1... | collective-permute-start | bytes 1179656 | tf_op jit(solution)/shard_map/ppermute | solution.py:252
  11.8 5.4 %collective-permute-done.top_ref = f32[384,256]{1,0:T(8,128)S(1)} collective-permute-done((f32[384,256]{1,0:T(8,128)}, f32[384,256]{1,0:T(8,128)S(1)}, u32[]{:S(2)}, u32[]{:S(2)}) %collective-permute-start) | collective-permute-done | bytes 393248 | tf_op jit(solution)/shard_map/ppermute | solution.py:252
  28.8 5.2 %collective-permute-done.1.top_ref = f32[384,256]{1,0:T(8,128)S(1)} collective-permute-done((f32[384,256]{1,0:T(8,128)S(1)}, f32[384,256]{1,0:T(8,128)S(1)}, u32[]{:S(2)}, u32[]{:S(2)}) %collective-permute-start.1) | collective-permute-done | bytes 393248 | tf_op jit(solution)/shard_map/ppermute | solution.py:256
  44.9 4.3 %collective-permute-start.8 = (f32[128,256]{1,0:T(8,128)S(1)}, f32[128,256]{1,0:T(8,128)S(1)}, u32[]{:S(2)}, u32[]{:S(2)}) collective-permute-start(f32[128,256]{1,0:T(8,128)S(1)} %get-tuple-element.117), channel_id=1, source_target_pairs={{0,1},{1,0},{2,3},{3,2},{4,5},{5,4},{6,7},{7,6},{8,9},{9,8},{10,11... | collective-permute-start | bytes 393224 | tf_op jit(solution)/shard_map/ppermute | solution.py:273
  50.2 3.7 %collective-permute-done.9.from_b = f32[128,256]{1,0:T(8,128)S(1)} collective-permute-done((f32[128,256]{1,0:T(8,128)S(1)}, f32[128,256]{1,0:T(8,128)S(1)}, u32[]{:S(2)}, u32[]{:S(2)}) %collective-permute-start.9) | collective-permute-done | bytes 131104 | tf_op jit(solution)/shard_map/ppermute | solution.py:272
  56.3 3.7 %collective-permute-done.11.from_b = f32[128,256]{1,0:T(8,128)S(1)} collective-permute-done((f32[128,256]{1,0:T(8,128)S(1)}, f32[128,256]{1,0:T(8,128)S(1)}, u32[]{:S(2)}, u32[]{:S(2)}) %collective-permute-start.11) | collective-permute-done | bytes 131104 | tf_op jit(solution)/shard_map/ppermute | solution.py:272
  62.4 3.7 %collective-permute-done.13.from_b = f32[128,256]{1,0:T(8,128)S(1)} collective-permute-done((f32[128,256]{1,0:T(8,128)S(1)}, f32[128,256]{1,0:T(8,128)S(1)}, u32[]{:S(2)}, u32[]{:S(2)}) %collective-permute-start.13) | collective-permute-done | bytes 131104 | tf_op jit(solution)/shard_map/ppermute | solution.py:272
  67.4 3.8 %collective-permute-done.14.state_ref = f32[128,256]{1,0:T(8,128)S(1)} collective-permute-done((f32[128,256]{1,0:T(8,128)S(1)}, f32[128,256]{1,0:T(8,128)S(1)}, u32[]{:S(2)}, u32[]{:S(2)}) %collective-permute-start.14) | collective-permute-done | bytes 131104 | tf_op jit(solution)/shard_map/ppermute | solution.py:269
  74.9 3.7 %collective-permute-done.16.from_b = f32[128,256]{1,0:T(8,128)S(1)} collective-permute-done((f32[128,256]{1,0:T(8,128)S(1)}, f32[128,256]{1,0:T(8,128)S(1)}, u32[]{:S(2)}, u32[]{:S(2)}) %collective-permute-start.16) | collective-permute-done | bytes 131104 | tf_op jit(solution)/shard_map/ppermute | solution.py:272
  81.0 3.7 %collective-permute-done.18.from_b = f32[128,256]{1,0:T(8,128)S(1)} collective-permute-done((f32[128,256]{1,0:T(8,128)S(1)}, f32[128,256]{1,0:T(8,128)S(1)}, u32[]{:S(2)}, u32[]{:S(2)}) %collective-permute-start.18) | collective-permute-done | bytes 131104 | tf_op jit(solution)/shard_map/ppermute | solution.py:272
  87.0 3.7 %collective-permute-done.20.from_b = f32[128,256]{1,0:T(8,128)S(1)} collective-permute-done((f32[128,256]{1,0:T(8,128)S(1)}, f32[128,256]{1,0:T(8,128)S(1)}, u32[]{:S(2)}, u32[]{:S(2)}) %collective-permute-start.20) | collective-permute-done | bytes 131104 | tf_op jit(solution)/shard_map/ppermute | solution.py:272
  93.1 3.7 %collective-permute-done.22.from_b = f32[128,256]{1,0:T(8,128)S(1)} collective-permute-done((f32[128,256]{1,0:T(8,128)S(1)}, f32[128,256]{1,0:T(8,128)S(1)}, u32[]{:S(2)}, u32[]{:S(2)}) %collective-permute-start.22) | collective-permute-done | bytes 131104 | tf_op jit(solution)/shard_map/ppermute | solution.py:272
  96.9 5.0 %collective-permute-done.23.state_ref = f32[128,256]{1,0:T(8,128)S(1)} collective-permute-done((f32[128,256]{1,0:T(8,128)S(1)}, f32[128,256]{1,0:T(8,128)S(1)}, u32[]{:S(2)}, u32[]{:S(2)}) %collective-permute-start.23) | collective-permute-done | bytes 131104 | tf_op jit(solution)/shard_map/ppermute | solution.py:269
  105.4 3.7 %collective-permute-done.25.from_b = f32[128,256]{1,0:T(8,128)S(1)} collective-permute-done((f32[128,256]{1,0:T(8,128)S(1)}, f32[128,256]{1,0:T(8,128)S(1)}, u32[]{:S(2)}, u32[]{:S(2)}) %collective-permute-start.25) | collective-permute-done | bytes 131104 | tf_op jit(solution)/shard_map/ppermute | solution.py:272
  111.5 3.7 %collective-permute-done.27.from_b = f32[128,256]{1,0:T(8,128)S(1)} collective-permute-done((f32[128,256]{1,0:T(8,128)S(1)}, f32[128,256]{1,0:T(8,128)S(1)}, u32[]{:S(2)}, u32[]{:S(2)}) %collective-permute-start.27) | collective-permute-done | bytes 131104 | tf_op jit(solution)/shard_map/ppermute | solution.py:272
  117.6 3.7 %collective-permute-done.29.from_b = f32[128,256]{1,0:T(8,128)S(1)} collective-permute-done((f32[128,256]{1,0:T(8,128)S(1)}, f32[128,256]{1,0:T(8,128)S(1)}, u32[]{:S(2)}, u32[]{:S(2)}) %collective-permute-start.29) | collective-permute-done | bytes 131104 | tf_op jit(solution)/shard_map/ppermute | solution.py:272
  123.7 3.7 %collective-permute-done.31.from_b = f32[128,256]{1,0:T(8,128)S(1)} collective-permute-done((f32[128,256]{1,0:T(8,128)S(1)}, f32[128,256]{1,0:T(8,128)S(1)}, u32[]{:S(2)}, u32[]{:S(2)}) %collective-permute-start.31) | collective-permute-done | bytes 131104 | tf_op jit(solution)/shard_map/ppermute | solution.py:272
  127.5 5.0 %collective-permute-done.32.state_ref = f32[128,256]{1,0:T(8,128)S(1)} collective-permute-done((f32[128,256]{1,0:T(8,128)S(1)}, f32[128,256]{1,0:T(8,128)S(1)}, u32[]{:S(2)}, u32[]{:S(2)}) %collective-permute-start.32) | collective-permute-done | bytes 131104 | tf_op jit(solution)/shard_map/ppermute | solution.py:269
  136.2 3.7 %collective-permute-done.34.from_b = f32[128,256]{1,0:T(8,128)S(1)} collective-permute-done((f32[128,256]{1,0:T(8,128)S(1)}, f32[128,256]{1,0:T(8,128)S(1)}, u32[]{:S(2)}, u32[]{:S(2)}) %collective-permute-start.34) | collective-permute-done | bytes 131104 | tf_op jit(solution)/shard_map/ppermute | solution.py:272
  142.3 3.7 %collective-permute-done.36.from_b = f32[128,256]{1,0:T(8,128)S(1)} collective-permute-done((f32[128,256]{1,0:T(8,128)S(1)}, f32[128,256]{1,0:T(8,128)S(1)}, u32[]{:S(2)}, u32[]{:S(2)}) %collective-permute-start.36) | collective-permute-done | bytes 131104 | tf_op jit(solution)/shard_map/ppermute | solution.py:272
  148.3 3.7 %collective-permute-done.38.from_b = f32[128,256]{1,0:T(8,128)S(1)} collective-permute-done((f32[128,256]{1,0:T(8,128)S(1)}, f32[128,256]{1,0:T(8,128)S(1)}, u32[]{:S(2)}, u32[]{:S(2)}) %collective-permute-start.38) | collective-permute-done | bytes 131104 | tf_op jit(solution)/shard_map/ppermute | solution.py:272
  154.4 3.7 %collective-permute-done.40.from_b = f32[128,256]{1,0:T(8,128)S(1)} collective-permute-done((f32[128,256]{1,0:T(8,128)S(1)}, f32[128,256]{1,0:T(8,128)S(1)}, u32[]{:S(2)}, u32[]{:S(2)}) %collective-permute-start.40) | collective-permute-done | bytes 131104 | tf_op jit(solution)/shard_map/ppermute | solution.py:272
  161.6 5.9 %collective-permute-done.41.refs_0_ = f32[128,256]{1,0:T(8,128)S(1)} collective-permute-done((f32[128,256]{1,0:T(8,128)S(1)}, f32[128,256]{1,0:T(8,128)S(1)}, u32[]{:S(2)}, u32[]{:S(2)}) %collective-permute-start.41) | collective-permute-done | bytes 131104 | tf_op jit(solution)/shard_map/ppermute | solution.py:293
  (113 shorter events, 68.6 us)
Async XLA Ops:
  5.5 11.7 %collective-permute-start = (f32[384,256]{1,0:T(8,128)}, f32[384,256]{1,0:T(8,128)S(1)}, u32[]{:S(2)}, u32[]{:S(2)}) collective-permute-start(f32[384,256]{1,0:T(8,128)} %get-tuple-element.102.top_ref), channel_id=1, source_target_pairs={{0,48},{16,0},{32,16},{48,32},{64,112},{80,64},{96,80},{112,96},{1... | collective-permute-start | bytes 1179656 | tf_op jit(solution)/shard_map/ppermute | solution.py:252
  9.2 11.4 %collective-permute-start.2 = (f32[384,256]{1,0:T(8,128)}, f32[384,256]{1,0:T(8,128)S(1)}, u32[]{:S(2)}, u32[]{:S(2)}) collective-permute-start(f32[384,256]{1,0:T(8,128)} %get-tuple-element.103.bottom_ref), channel_id=1, source_target_pairs={{0,16},{16,32},{32,48},{48,0},{64,80},{80,96},{96,112},{112,64},{1... | collective-permute-start | bytes 1179656 | tf_op jit(solution)/shard_map/ppermute | solution.py:253
  9.2 16.5 %collective-permute-start.5 = (f32[384,256]{1,0:T(8,128)}, f32[384,256]{1,0:T(8,128)S(1)}, u32[]{:S(2)}, u32[]{:S(2)}) collective-permute-start(f32[384,256]{1,0:T(8,128)} %get-tuple-element.103.bottom_ref), channel_id=1, source_target_pairs={{0,48},{16,0},{32,16},{48,32},{64,112},{80,64},{96,80},{112,96},{1... | collective-permute-start | bytes 1179656 | tf_op jit(solution)/shard_map/ppermute | solution.py:254
  11.8 16.8 %collective-permute-start.4 = (f32[384,256]{1,0:T(8,128)}, f32[384,256]{1,0:T(8,128)S(1)}, u32[]{:S(2)}, u32[]{:S(2)}) collective-permute-start(f32[384,256]{1,0:T(8,128)} %get-tuple-element.102.top_ref), channel_id=1, source_target_pairs={{0,16},{16,32},{32,48},{48,0},{64,80},{80,96},{96,112},{112,64},{1... | collective-permute-start | bytes 1179656 | tf_op jit(solution)/shard_map/ppermute | solution.py:255
  17.3 16.7 %collective-permute-start.1 = (f32[384,256]{1,0:T(8,128)S(1)}, f32[384,256]{1,0:T(8,128)S(1)}, u32[]{:S(2)}, u32[]{:S(2)}) collective-permute-start(f32[384,256]{1,0:T(8,128)S(1)} %collective-permute-done.top_ref), channel_id=1, source_target_pairs={{0,48},{16,0},{32,16},{48,32},{64,112},{80,64},{96,80},{112,96},{1... | collective-permute-start | bytes 1179656 | tf_op jit(solution)/shard_map/ppermute | solution.py:256
  20.6 16.5 %collective-permute-start.3 = (f32[384,256]{1,0:T(8,128)S(1)}, f32[384,256]{1,0:T(8,128)S(1)}, u32[]{:S(2)}, u32[]{:S(2)}) collective-permute-start(f32[384,256]{1,0:T(8,128)S(1)} %collective-permute-done.2.bottom_ref), channel_id=1, source_target_pairs={{0,16},{16,32},{32,48},{48,0},{64,80},{80,96},{96,112},{112,64},{1... | collective-permute-start | bytes 1179656 | tf_op jit(solution)/shard_map/ppermute | solution.py:257
  44.9 5.3 %collective-permute-start.8 = (f32[128,256]{1,0:T(8,128)S(1)}, f32[128,256]{1,0:T(8,128)S(1)}, u32[]{:S(2)}, u32[]{:S(2)}) collective-permute-start(f32[128,256]{1,0:T(8,128)S(1)} %get-tuple-element.117), channel_id=1, source_target_pairs={{0,1},{1,0},{2,3},{3,2},{4,5},{5,4},{6,7},{7,6},{8,9},{9,8},{10,11... | collective-permute-start | bytes 393224 | tf_op jit(solution)/shard_map/ppermute | solution.py:273
  49.3 4.7 %collective-permute-start.9 = (f32[128,256]{1,0:T(8,128)S(1)}, f32[128,256]{1,0:T(8,128)S(1)}, u32[]{:S(2)}, u32[]{:S(2)}) collective-permute-start(f32[128,256]{1,0:T(8,128)S(1)} %get-tuple-element.118), channel_id=1, source_target_pairs={{0,15},{1,2},{2,1},{3,4},{4,3},{5,6},{6,5},{7,8},{8,7},{9,10},{10,... | collective-permute-start | bytes 393224 | tf_op jit(solution)/shard_map/ppermute | solution.py:272
  55.3 4.7 %collective-permute-start.11 = (f32[128,256]{1,0:T(8,128)S(1)}, f32[128,256]{1,0:T(8,128)S(1)}, u32[]{:S(2)}, u32[]{:S(2)}) collective-permute-start(f32[128,256]{1,0:T(8,128)S(1)} %get-tuple-element.123), channel_id=1, source_target_pairs={{0,15},{1,2},{2,1},{3,4},{4,3},{5,6},{6,5},{7,8},{8,7},{9,10},{10,... | collective-permute-start | bytes 393224 | tf_op jit(solution)/shard_map/ppermute | solution.py:272
  61.4 4.7 %collective-permute-start.13 = (f32[128,256]{1,0:T(8,128)S(1)}, f32[128,256]{1,0:T(8,128)S(1)}, u32[]{:S(2)}, u32[]{:S(2)}) collective-permute-start(f32[128,256]{1,0:T(8,128)S(1)} %get-tuple-element.128), channel_id=1, source_target_pairs={{0,15},{1,2},{2,1},{3,4},{4,3},{5,6},{6,5},{7,8},{8,7},{9,10},{10,... | collective-permute-start | bytes 393224 | tf_op jit(solution)/shard_map/ppermute | solution.py:272
  66.1 5.1 %collective-permute-start.14 = (f32[128,256]{1,0:T(8,128)S(1)}, f32[128,256]{1,0:T(8,128)S(1)}, u32[]{:S(2)}, u32[]{:S(2)}) collective-permute-start(f32[128,256]{1,0:T(8,128)S(1)} %get-tuple-element.130), channel_id=1, source_target_pairs={{0,64},{16,80},{32,96},{48,112},{64,128},{80,144},{96,160},{112,17... | collective-permute-start | bytes 393224 | tf_op jit(solution)/shard_map/ppermute | solution.py:269
  73.9 4.7 %collective-permute-start.16 = (f32[128,256]{1,0:T(8,128)S(1)}, f32[128,256]{1,0:T(8,128)S(1)}, u32[]{:S(2)}, u32[]{:S(2)}) collective-permute-start(f32[128,256]{1,0:T(8,128)S(1)} %get-tuple-element.132), channel_id=1, source_target_pairs={{0,15},{1,2},{2,1},{3,4},{4,3},{5,6},{6,5},{7,8},{8,7},{9,10},{10,... | collective-permute-start | bytes 393224 | tf_op jit(solution)/shard_map/ppermute | solution.py:272
  80.0 4.7 %collective-permute-start.18 = (f32[128,256]{1,0:T(8,128)S(1)}, f32[128,256]{1,0:T(8,128)S(1)}, u32[]{:S(2)}, u32[]{:S(2)}) collective-permute-start(f32[128,256]{1,0:T(8,128)S(1)} %get-tuple-element.137), channel_id=1, source_target_pairs={{0,15},{1,2},{2,1},{3,4},{4,3},{5,6},{6,5},{7,8},{8,7},{9,10},{10,... | collective-permute-start | bytes 393224 | tf_op jit(solution)/shard_map/ppermute | solution.py:272
  96.8 5.1 %collective-permute-start.23 = (f32[128,256]{1,0:T(8,128)S(1)}, f32[128,256]{1,0:T(8,128)S(1)}, u32[]{:S(2)}, u32[]{:S(2)}) collective-permute-start(f32[128,256]{1,0:T(8,128)S(1)} %get-tuple-element.149), channel_id=1, source_target_pairs={{0,64},{16,80},{32,96},{48,112},{64,128},{80,144},{96,160},{112,17... | collective-permute-start | bytes 393224 | tf_op jit(solution)/shard_map/ppermute | solution.py:269
  104.5 4.7 %collective-permute-start.25 = (f32[128,256]{1,0:T(8,128)S(1)}, f32[128,256]{1,0:T(8,128)S(1)}, u32[]{:S(2)}, u32[]{:S(2)}) collective-permute-start(f32[128,256]{1,0:T(8,128)S(1)} %get-tuple-element.151), channel_id=1, source_target_pairs={{0,15},{1,2},{2,1},{3,4},{4,3},{5,6},{6,5},{7,8},{8,7},{9,10},{10,... | collective-permute-start | bytes 393224 | tf_op jit(solution)/shard_map/ppermute | solution.py:272
  110.5 4.7 %collective-permute-start.27 = (f32[128,256]{1,0:T(8,128)S(1)}, f32[128,256]{1,0:T(8,128)S(1)}, u32[]{:S(2)}, u32[]{:S(2)}) collective-permute-start(f32[128,256]{1,0:T(8,128)S(1)} %get-tuple-element.156), channel_id=1, source_target_pairs={{0,15},{1,2},{2,1},{3,4},{4,3},{5,6},{6,5},{7,8},{8,7},{9,10},{10,... | collective-permute-start | bytes 393224 | tf_op jit(solution)/shard_map/ppermute | solution.py:272
  116.6 4.7 %collective-permute-start.29 = (f32[128,256]{1,0:T(8,128)S(1)}, f32[128,256]{1,0:T(8,128)S(1)}, u32[]{:S(2)}, u32[]{:S(2)}) collective-permute-start(f32[128,256]{1,0:T(8,128)S(1)} %get-tuple-element.161), channel_id=1, source_target_pairs={{0,15},{1,2},{2,1},{3,4},{4,3},{5,6},{6,5},{7,8},{8,7},{9,10},{10,... | collective-permute-start | bytes 393224 | tf_op jit(solution)/shard_map/ppermute | solution.py:272
  122.7 4.7 %collective-permute-start.31 = (f32[128,256]{1,0:T(8,128)S(1)}, f32[128,256]{1,0:T(8,128)S(1)}, u32[]{:S(2)}, u32[]{:S(2)}) collective-permute-start(f32[128,256]{1,0:T(8,128)S(1)} %get-tuple-element.166), channel_id=1, source_target_pairs={{0,15},{1,2},{2,1},{3,4},{4,3},{5,6},{6,5},{7,8},{8,7},{9,10},{10,... | collective-permute-start | bytes 393224 | tf_op jit(solution)/shard_map/ppermute | solution.py:272
  127.4 5.1 %collective-permute-start.32 = (f32[128,256]{1,0:T(8,128)S(1)}, f32[128,256]{1,0:T(8,128)S(1)}, u32[]{:S(2)}, u32[]{:S(2)}) collective-permute-start(f32[128,256]{1,0:T(8,128)S(1)} %get-tuple-element.168), channel_id=1, source_target_pairs={{0,64},{16,80},{32,96},{48,112},{64,128},{80,144},{96,160},{112,17... | collective-permute-start | bytes 393224 | tf_op jit(solution)/shard_map/ppermute | solution.py:269
  135.2 4.7 %collective-permute-start.34 = (f32[128,256]{1,0:T(8,128)S(1)}, f32[128,256]{1,0:T(8,128)S(1)}, u32[]{:S(2)}, u32[]{:S(2)}) collective-permute-start(f32[128,256]{1,0:T(8,128)S(1)} %get-tuple-element.170), channel_id=1, source_target_pairs={{0,15},{1,2},{2,1},{3,4},{4,3},{5,6},{6,5},{7,8},{8,7},{9,10},{10,... | collective-permute-start | bytes 393224 | tf_op jit(solution)/shard_map/ppermute | solution.py:272
  147.4 4.7 %collective-permute-start.38 = (f32[128,256]{1,0:T(8,128)S(1)}, f32[128,256]{1,0:T(8,128)S(1)}, u32[]{:S(2)}, u32[]{:S(2)}) collective-permute-start(f32[128,256]{1,0:T(8,128)S(1)} %get-tuple-element.180), channel_id=1, source_target_pairs={{0,15},{1,2},{2,1},{3,4},{4,3},{5,6},{6,5},{7,8},{8,7},{9,10},{10,... | collective-permute-start | bytes 393224 | tf_op jit(solution)/shard_map/ppermute | solution.py:272
  158.8 8.7 %collective-permute-start.41 = (f32[128,256]{1,0:T(8,128)S(1)}, f32[128,256]{1,0:T(8,128)S(1)}, u32[]{:S(2)}, u32[]{:S(2)}) collective-permute-start(f32[128,256]{1,0:T(8,128)S(1)} %get-tuple-element.188), channel_id=1, source_target_pairs={{0,16},{16,32},{32,48},{48,0},{64,80},{80,96},{96,112},{112,64},{1... | collective-permute-start | bytes 393224 | tf_op jit(solution)/shard_map/ppermute | solution.py:293
  158.9 8.6 %collective-permute-start.42 = (f32[128,256]{1,0:T(8,128)S(1)}, f32[128,256]{1,0:T(8,128)S(1)}, u32[]{:S(2)}, u32[]{:S(2)}) collective-permute-start(f32[128,256]{1,0:T(8,128)S(1)} %get-tuple-element.189), channel_id=1, source_target_pairs={{0,32},{16,48},{32,0},{48,16},{64,96},{80,112},{96,64},{112,80},{1... | collective-permute-start | bytes 393224 | tf_op jit(solution)/shard_map/ppermute | solution.py:293
  160.1 7.4 %collective-permute-start.43 = (f32[128,256]{1,0:T(8,128)S(1)}, f32[128,256]{1,0:T(8,128)S(1)}, u32[]{:S(2)}, u32[]{:S(2)}) collective-permute-start(f32[128,256]{1,0:T(8,128)S(1)} %get-tuple-element.190), channel_id=1, source_target_pairs={{0,48},{16,0},{32,16},{48,32},{64,112},{80,64},{96,80},{112,96},{1... | collective-permute-start | bytes 393224 | tf_op jit(solution)/shard_map/ppermute | solution.py:293
  (23 other events, 63.0 us)

commit v3 on v2

--- a/solution.py
+++ b/solution.py
@@ -167,12 +167,10 @@
         out[...] = times(state, high_ref[where], low_ref[where])
 
 
-def edge_kernel(y_ref, edge_ref, high_ref, low_ref, state_ref, out_a, out_b):
+def edge_kernel(y_ref, edge_ref, state_ref):
     slab = state_ref.shape[0]
     at = pl.multiple_of(y_ref[0] * slab, slab)
-    state = edge_ref[pl.ds(at, slab), :].astype(jnp.float32)
-    state_ref[...] = state
-    away_of(0, state, high_ref, low_ref, out_a, out_b)
+    state_ref[...] = edge_ref[pl.ds(at, slab), :].astype(jnp.float32)
 
 
 def away_kernel(state_ref, high_ref, low_ref, out_a, out_b):
@@ -206,10 +204,12 @@
     out_ref[...] = times(state, high_ref[where], low_ref[where])
 
 
-def sum_kernel(phase, x_ref, inner_ref, stay_ref, from_a, from_b, old_ref, state_ref, kept_ref):
-    state = summed(inner_ref, stay_ref, from_a, from_b)
-    state_ref[...] = state
-    keep_at(phase, GROUP - 1, x_ref, state, kept_ref)
+def sum_kernel(inner_ref, stay_ref, from_a, from_b, state_ref):
+    state_ref[...] = summed(inner_ref, stay_ref, from_a, from_b)
+
+
+def keep_kernel(phase, x_ref, state_ref, old_ref, kept_ref):
+    keep_at(phase, GROUP - 1, x_ref, state_ref[...], kept_ref)
 
 
 def pick_kernel(y_ref, kept_ref, *outs):
@@ -253,21 +253,20 @@
     down_bottom = lax.ppermute(bottom, "site", ring(1))
     up_bottom = lax.ppermute(bottom, "site", ring(-1))
     down_top = lax.ppermute(top, "site", ring(1))
+    state, = call(edge_kernel, (state_shape,), (info[Y],), (left_edge,), name="edge")
+    placed = place(info, 0, top, bottom, ())
+    placed, state, up_top, down_bottom = lax.optimization_barrier((placed, state, up_top, down_bottom))
     far_top = lax.ppermute(up_top, "site", ring(-1))
     far_bottom = lax.ppermute(down_bottom, "site", ring(1))
-    placed = place(info, 0, top, bottom, ())
     placed = place(info, 1, up_top, up_bottom, placed)
     placed = place(info, 3, down_top, down_bottom, placed)
     placed = place(info, 2, far_top, far_bottom, placed)
 
-    state, out_a, out_b = call(
-        edge_kernel, (state_shape,) * 3, (info[Y],), (left_edge, *placed), 2, name="away"
-    )
     kept = None
     for phase in range(sites // GROUP):
         if phase:
             state = lax.ppermute(state, "site", hop)
-            out_a, out_b = call(away_kernel, (state_shape,) * 2, (), (state, *placed), 2, name="away")
+        out_a, out_b = call(away_kernel, (state_shape,) * 2, (), (state, *placed), 2, name="away")
         for site in range(GROUP):
             from_b = lax.ppermute(out_b, "sector", across)
             from_a = lax.ppermute(out_a, "sector", inside)
@@ -284,10 +283,9 @@
                 arrays = (stay, from_a, from_b, *placed)
                 state, out_a, out_b = call(kernel, (state_shape,) * 3, (info[INNER],), arrays, 2, name="sum_away")
             else:
-                kernel = functools.partial(sum_kernel, phase)
-                arrays = (stay, from_a, from_b, kept)
-                scalars = (info[X], info[INNER])
-                state, kept = call(kernel, (state_shape, kept_shape), scalars, arrays, 0, {5: 1}, "sum")
+                state, = call(sum_kernel, (state_shape,), (info[INNER],), (stay, from_a, from_b), name="sum")
+                kernel = functools.partial(keep_kernel, phase)
+                kept, = call(kernel, (kept_shape,), (info[X],), (state, kept), 0, {2: 0}, "keep")
 
     sent = call(pick_kernel, (state_shape,) * (GROUP - 1), (info[Y],), (kept,), name="pick")
     came = [lax.ppermute(out, "site", ring(by + 1)) for by, out in enumerate(sent)]

time: 169 us -> 167 us (0.988)
  starting transfers between devices: 41.1 us -> 39.3 us
    ppermute x1, waiting for transfers between devices: 0.01 us -> 2.98 us  [local(): down_bottom = lax.ppermute(bottom, 'site', ring(1))]
    ppermute x1, starting transfers between devices: 3.31 us -> 0.33 us  [local(): far_top = lax.ppermute(up_top, 'site', ring(-1))]
    ppermute x1, waiting for transfers between devices: 5.41 us -> 3.22 us  [local(): up_top = lax.ppermute(top, 'site', ring(-1))]
    pallas_call x42 -> x47, Pallas kernels: 10 us -> 9.43 us  [call(): pl.pallas_call(kernel, out_shape=shapes, in_specs=[SMEM] * len(scalars) +...]
  transfers between devices with their start and end apart: 44 -> 44, of which waited for: 40 -> 41; matrix products, arithmetic and copies ran while one was open for 0% -> 0% of each run, Pallas kernels for 2% -> 2%
where the time goes in v3:
time: 167 us
  waiting for transfers between devices  110 us (66%)
  starting transfers between devices  39.3 us (24%)
  Pallas kernels  15 us (9%)
  local copies, waits for them, and re-layouts  1.99 us (1%)
    ppermute x16, waiting for transfers between devices, local(): from_b = lax.ppermute(out_b, 'sector', across)  58 us
    ppermute x16, starting transfers between devices, local(): from_a = lax.ppermute(out_a, 'sector', inside)  25.6 us
    ppermute x3, waiting for transfers between devices, local(): state = lax.ppermute(state, 'site', hop)  13.8 us
    ppermute x16, waiting for transfers between devices, local(): from_a = lax.ppermute(out_a, 'sector', inside)  11.2 us
    pallas_call x47, Pallas kernels, call(): pl.pallas_call(kernel, out_shape=shapes, in_specs=[SMEM] * len(scalars) +...  9.43 us
    ppermute x3, waiting for transfers between devices, local(): lax.ppermute(out, 'site', ring(by + 1))  5.9 us
    pallas_call x1, Pallas kernels, transfer(): pl.pallas_call(transfer_kernel, out_shape=(half, half), in_specs=[SMEM] *...  5.61 us
    ppermute x1, waiting for transfers between devices, local(): far_top = lax.ppermute(up_top, 'site', ring(-1))  5.2 us
  transfers between devices with their start and end apart: 44, of which 41 were waited for; matrix products, arithmetic and copies ran while one was open for 0% of the time, Pallas kernels for 2%

profile of v3, /device:TPU:1, one launch (start us, length us, event | category | flops | bytes accessed | tf_op | source)
XLA Modules:
  0.0 167.0 jit_solution(2410056996811796991)
XLA Ops:
  0.0 5.6 %transfer.1 = (f32[384,256]{1,0:T(8,128)}, f32[384,256]{1,0:T(8,128)}) custom-call(s32[1]{0:T(128)} %bitcast.x_ref, s32[1]{0:T(128)} %bitcast.1.y_ref, s32[1]{0:T(128)} %bitcast.2.sign_ref, s32[1]{0:T(128)} %bitcast.3.inner_ref, s32[8]{0:T(128)} %bitcast.13, bf16[8,32]{1,0:T(8,128)(2,1)} %bitcast.12, bf16[8192,256]{1,0:T(8,128)(2,1)} %bitcast.10, ...), custom_call_target="tpu_custom_call" | custom-call | tf_op jit(solution)/shard_map/transfer/pallas_call | solution.py:94
  5.6 3.6 %collective-permute-start = (f32[384,256]{1,0:T(8,128)}, f32[384,256]{1,0:T(8,128)S(1)}, u32[]{:S(2)}, u32[]{:S(2)}) collective-permute-start(f32[384,256]{1,0:T(8,128)} %get-tuple-element.99.top_ref), channel_id=1, source_target_pairs={{0,48},{16,0},{32,16},{48,32},{64,112},{80,64},{96,80},{112,96},{1... | collective-permute-start | bytes 1179656 | tf_op jit(solution)/shard_map/ppermute | solution.py:252
  21.8 4.0 %collective-permute-done.5.bottom_ref = f32[384,256]{1,0:T(8,128)S(1)} collective-permute-done((f32[384,256]{1,0:T(8,128)}, f32[384,256]{1,0:T(8,128)S(1)}, u32[]{:S(2)}, u32[]{:S(2)}) %collective-permute-start.5) | collective-permute-done | bytes 393248 | tf_op jit(solution)/shard_map/ppermute | solution.py:254
  28.9 5.2 %collective-permute-done.2.top_ref = f32[384,256]{1,0:T(8,128)S(1)} collective-permute-done((f32[384,256]{1,0:T(8,128)S(1)}, f32[384,256]{1,0:T(8,128)S(1)}, u32[]{:S(2)}, u32[]{:S(2)}) %collective-permute-start.2) | collective-permute-done | bytes 393248 | tf_op jit(solution)/shard_map/ppermute | solution.py:259
  44.2 4.3 %collective-permute-start.8 = (f32[128,256]{1,0:T(8,128)S(1)}, f32[128,256]{1,0:T(8,128)S(1)}, u32[]{:S(2)}, u32[]{:S(2)}) collective-permute-start(f32[128,256]{1,0:T(8,128)S(1)} %get-tuple-element.118), channel_id=1, source_target_pairs={{0,1},{1,0},{2,3},{3,2},{4,5},{5,4},{6,7},{7,6},{8,9},{9,8},{10,11... | collective-permute-start | bytes 393224 | tf_op jit(solution)/shard_map/ppermute | solution.py:272
  49.5 3.7 %collective-permute-done.9.from_b = f32[128,256]{1,0:T(8,128)S(1)} collective-permute-done((f32[128,256]{1,0:T(8,128)S(1)}, f32[128,256]{1,0:T(8,128)S(1)}, u32[]{:S(2)}, u32[]{:S(2)}) %collective-permute-start.9) | collective-permute-done | bytes 131104 | tf_op jit(solution)/shard_map/ppermute | solution.py:271
  55.6 3.7 %collective-permute-done.11.from_b = f32[128,256]{1,0:T(8,128)S(1)} collective-permute-done((f32[128,256]{1,0:T(8,128)S(1)}, f32[128,256]{1,0:T(8,128)S(1)}, u32[]{:S(2)}, u32[]{:S(2)}) %collective-permute-start.11) | collective-permute-done | bytes 131104 | tf_op jit(solution)/shard_map/ppermute | solution.py:271
  61.7 3.7 %collective-permute-done.13.from_b = f32[128,256]{1,0:T(8,128)S(1)} collective-permute-done((f32[128,256]{1,0:T(8,128)S(1)}, f32[128,256]{1,0:T(8,128)S(1)}, u32[]{:S(2)}, u32[]{:S(2)}) %collective-permute-start.13) | collective-permute-done | bytes 131104 | tf_op jit(solution)/shard_map/ppermute | solution.py:271
  66.7 3.8 %collective-permute-done.14.state_ref = f32[128,256]{1,0:T(8,128)S(1)} collective-permute-done((f32[128,256]{1,0:T(8,128)S(1)}, f32[128,256]{1,0:T(8,128)S(1)}, u32[]{:S(2)}, u32[]{:S(2)}) %collective-permute-start.14) | collective-permute-done | bytes 131104 | tf_op jit(solution)/shard_map/ppermute | solution.py:268
  74.2 3.7 %collective-permute-done.16.from_b = f32[128,256]{1,0:T(8,128)S(1)} collective-permute-done((f32[128,256]{1,0:T(8,128)S(1)}, f32[128,256]{1,0:T(8,128)S(1)}, u32[]{:S(2)}, u32[]{:S(2)}) %collective-permute-start.16) | collective-permute-done | bytes 131104 | tf_op jit(solution)/shard_map/ppermute | solution.py:271
  80.2 3.7 %collective-permute-done.18.from_b = f32[128,256]{1,0:T(8,128)S(1)} collective-permute-done((f32[128,256]{1,0:T(8,128)S(1)}, f32[128,256]{1,0:T(8,128)S(1)}, u32[]{:S(2)}, u32[]{:S(2)}) %collective-permute-start.18) | collective-permute-done | bytes 131104 | tf_op jit(solution)/shard_map/ppermute | solution.py:271
  86.3 3.7 %collective-permute-done.20.from_b = f32[128,256]{1,0:T(8,128)S(1)} collective-permute-done((f32[128,256]{1,0:T(8,128)S(1)}, f32[128,256]{1,0:T(8,128)S(1)}, u32[]{:S(2)}, u32[]{:S(2)}) %collective-permute-start.20) | collective-permute-done | bytes 131104 | tf_op jit(solution)/shard_map/ppermute | solution.py:271
  92.4 3.7 %collective-permute-done.22.from_b = f32[128,256]{1,0:T(8,128)S(1)} collective-permute-done((f32[128,256]{1,0:T(8,128)S(1)}, f32[128,256]{1,0:T(8,128)S(1)}, u32[]{:S(2)}, u32[]{:S(2)}) %collective-permute-start.22) | collective-permute-done | bytes 131104 | tf_op jit(solution)/shard_map/ppermute | solution.py:271
  96.2 5.0 %collective-permute-done.23.state_ref = f32[128,256]{1,0:T(8,128)S(1)} collective-permute-done((f32[128,256]{1,0:T(8,128)S(1)}, f32[128,256]{1,0:T(8,128)S(1)}, u32[]{:S(2)}, u32[]{:S(2)}) %collective-permute-start.23) | collective-permute-done | bytes 131104 | tf_op jit(solution)/shard_map/ppermute | solution.py:268
  104.7 3.7 %collective-permute-done.25.from_b = f32[128,256]{1,0:T(8,128)S(1)} collective-permute-done((f32[128,256]{1,0:T(8,128)S(1)}, f32[128,256]{1,0:T(8,128)S(1)}, u32[]{:S(2)}, u32[]{:S(2)}) %collective-permute-start.25) | collective-permute-done | bytes 131104 | tf_op jit(solution)/shard_map/ppermute | solution.py:271
  110.8 3.7 %collective-permute-done.27.from_b = f32[128,256]{1,0:T(8,128)S(1)} collective-permute-done((f32[128,256]{1,0:T(8,128)S(1)}, f32[128,256]{1,0:T(8,128)S(1)}, u32[]{:S(2)}, u32[]{:S(2)}) %collective-permute-start.27) | collective-permute-done | bytes 131104 | tf_op jit(solution)/shard_map/ppermute | solution.py:271
  116.9 3.7 %collective-permute-done.29.from_b = f32[128,256]{1,0:T(8,128)S(1)} collective-permute-done((f32[128,256]{1,0:T(8,128)S(1)}, f32[128,256]{1,0:T(8,128)S(1)}, u32[]{:S(2)}, u32[]{:S(2)}) %collective-permute-start.29) | collective-permute-done | bytes 131104 | tf_op jit(solution)/shard_map/ppermute | solution.py:271
  122.9 3.7 %collective-permute-done.31.from_b = f32[128,256]{1,0:T(8,128)S(1)} collective-permute-done((f32[128,256]{1,0:T(8,128)S(1)}, f32[128,256]{1,0:T(8,128)S(1)}, u32[]{:S(2)}, u32[]{:S(2)}) %collective-permute-start.31) | collective-permute-done | bytes 131104 | tf_op jit(solution)/shard_map/ppermute | solution.py:271
  126.8 5.0 %collective-permute-done.32.state_ref = f32[128,256]{1,0:T(8,128)S(1)} collective-permute-done((f32[128,256]{1,0:T(8,128)S(1)}, f32[128,256]{1,0:T(8,128)S(1)}, u32[]{:S(2)}, u32[]{:S(2)}) %collective-permute-start.32) | collective-permute-done | bytes 131104 | tf_op jit(solution)/shard_map/ppermute | solution.py:268
  135.5 3.7 %collective-permute-done.34.from_b = f32[128,256]{1,0:T(8,128)S(1)} collective-permute-done((f32[128,256]{1,0:T(8,128)S(1)}, f32[128,256]{1,0:T(8,128)S(1)}, u32[]{:S(2)}, u32[]{:S(2)}) %collective-permute-start.34) | collective-permute-done | bytes 131104 | tf_op jit(solution)/shard_map/ppermute | solution.py:271
  141.6 3.7 %collective-permute-done.36.from_b = f32[128,256]{1,0:T(8,128)S(1)} collective-permute-done((f32[128,256]{1,0:T(8,128)S(1)}, f32[128,256]{1,0:T(8,128)S(1)}, u32[]{:S(2)}, u32[]{:S(2)}) %collective-permute-start.36) | collective-permute-done | bytes 131104 | tf_op jit(solution)/shard_map/ppermute | solution.py:271
  147.6 3.7 %collective-permute-done.38.from_b = f32[128,256]{1,0:T(8,128)S(1)} collective-permute-done((f32[128,256]{1,0:T(8,128)S(1)}, f32[128,256]{1,0:T(8,128)S(1)}, u32[]{:S(2)}, u32[]{:S(2)}) %collective-permute-start.38) | collective-permute-done | bytes 131104 | tf_op jit(solution)/shard_map/ppermute | solution.py:271
  153.7 3.7 %collective-permute-done.40.from_b = f32[128,256]{1,0:T(8,128)S(1)} collective-permute-done((f32[128,256]{1,0:T(8,128)S(1)}, f32[128,256]{1,0:T(8,128)S(1)}, u32[]{:S(2)}, u32[]{:S(2)}) %collective-permute-start.40) | collective-permute-done | bytes 131104 | tf_op jit(solution)/shard_map/ppermute | solution.py:271
  160.2 5.9 %collective-permute-done.41.refs_0_ = f32[128,256]{1,0:T(8,128)S(1)} collective-permute-done((f32[128,256]{1,0:T(8,128)S(1)}, f32[128,256]{1,0:T(8,128)S(1)}, u32[]{:S(2)}, u32[]{:S(2)}) %collective-permute-start.41) | collective-permute-done | bytes 131104 | tf_op jit(solution)/shard_map/ppermute | solution.py:291
  (118 shorter events, 68.6 us)
Async XLA Ops:
  5.6 11.7 %collective-permute-start = (f32[384,256]{1,0:T(8,128)}, f32[384,256]{1,0:T(8,128)S(1)}, u32[]{:S(2)}, u32[]{:S(2)}) collective-permute-start(f32[384,256]{1,0:T(8,128)} %get-tuple-element.99.top_ref), channel_id=1, source_target_pairs={{0,48},{16,0},{32,16},{48,32},{64,112},{80,64},{96,80},{112,96},{1... | collective-permute-start | bytes 1179656 | tf_op jit(solution)/shard_map/ppermute | solution.py:252
  9.3 11.1 %collective-permute-start.1 = (f32[384,256]{1,0:T(8,128)}, f32[384,256]{1,0:T(8,128)S(1)}, u32[]{:S(2)}, u32[]{:S(2)}) collective-permute-start(f32[384,256]{1,0:T(8,128)} %get-tuple-element.100.bottom_ref), channel_id=1, source_target_pairs={{0,16},{16,32},{32,48},{48,0},{64,80},{80,96},{96,112},{112,64},{1... | collective-permute-start | bytes 1179656 | tf_op jit(solution)/shard_map/ppermute | solution.py:253
  9.3 19.5 %collective-permute-start.4 = (f32[384,256]{1,0:T(8,128)}, f32[384,256]{1,0:T(8,128)S(1)}, u32[]{:S(2)}, u32[]{:S(2)}) collective-permute-start(f32[384,256]{1,0:T(8,128)} %get-tuple-element.99.top_ref), channel_id=1, source_target_pairs={{0,16},{16,32},{32,48},{48,0},{64,80},{80,96},{96,112},{112,64},{1... | collective-permute-start | bytes 1179656 | tf_op jit(solution)/shard_map/ppermute | solution.py:255
  9.3 16.5 %collective-permute-start.5 = (f32[384,256]{1,0:T(8,128)}, f32[384,256]{1,0:T(8,128)S(1)}, u32[]{:S(2)}, u32[]{:S(2)}) collective-permute-start(f32[384,256]{1,0:T(8,128)} %get-tuple-element.100.bottom_ref), channel_id=1, source_target_pairs={{0,48},{16,0},{32,16},{48,32},{64,112},{80,64},{96,80},{112,96},{1... | collective-permute-start | bytes 1179656 | tf_op jit(solution)/shard_map/ppermute | solution.py:254
  20.3 13.8 %collective-permute-start.2 = (f32[384,256]{1,0:T(8,128)S(1)}, f32[384,256]{1,0:T(8,128)S(1)}, u32[]{:S(2)}, u32[]{:S(2)}) collective-permute-start(f32[384,256]{1,0:T(8,128)S(1)} %collective-permute-done.top_ref), channel_id=1, source_target_pairs={{0,48},{16,0},{32,16},{48,32},{64,112},{80,64},{96,80},{112,96},{1... | collective-permute-start | bytes 1179656 | tf_op jit(solution)/shard_map/ppermute | solution.py:259
  20.7 16.5 %collective-permute-start.3 = (f32[384,256]{1,0:T(8,128)S(1)}, f32[384,256]{1,0:T(8,128)S(1)}, u32[]{:S(2)}, u32[]{:S(2)}) collective-permute-start(f32[384,256]{1,0:T(8,128)S(1)} %collective-permute-done.1.bottom_ref), channel_id=1, source_target_pairs={{0,16},{16,32},{32,48},{48,0},{64,80},{80,96},{96,112},{112,64},{1... | collective-permute-start | bytes 1179656 | tf_op jit(solution)/shard_map/ppermute | solution.py:260
  44.2 5.3 %collective-permute-start.8 = (f32[128,256]{1,0:T(8,128)S(1)}, f32[128,256]{1,0:T(8,128)S(1)}, u32[]{:S(2)}, u32[]{:S(2)}) collective-permute-start(f32[128,256]{1,0:T(8,128)S(1)} %get-tuple-element.118), channel_id=1, source_target_pairs={{0,1},{1,0},{2,3},{3,2},{4,5},{5,4},{6,7},{7,6},{8,9},{9,8},{10,11... | collective-permute-start | bytes 393224 | tf_op jit(solution)/shard_map/ppermute | solution.py:272
  48.5 4.7 %collective-permute-start.9 = (f32[128,256]{1,0:T(8,128)S(1)}, f32[128,256]{1,0:T(8,128)S(1)}, u32[]{:S(2)}, u32[]{:S(2)}) collective-permute-start(f32[128,256]{1,0:T(8,128)S(1)} %get-tuple-element.119), channel_id=1, source_target_pairs={{0,15},{1,2},{2,1},{3,4},{4,3},{5,6},{6,5},{7,8},{8,7},{9,10},{10,... | collective-permute-start | bytes 393224 | tf_op jit(solution)/shard_map/ppermute | solution.py:271
  54.6 4.7 %collective-permute-start.11 = (f32[128,256]{1,0:T(8,128)S(1)}, f32[128,256]{1,0:T(8,128)S(1)}, u32[]{:S(2)}, u32[]{:S(2)}) collective-permute-start(f32[128,256]{1,0:T(8,128)S(1)} %get-tuple-element.124), channel_id=1, source_target_pairs={{0,15},{1,2},{2,1},{3,4},{4,3},{5,6},{6,5},{7,8},{8,7},{9,10},{10,... | collective-permute-start | bytes 393224 | tf_op jit(solution)/shard_map/ppermute | solution.py:271
  60.7 4.7 %collective-permute-start.13 = (f32[128,256]{1,0:T(8,128)S(1)}, f32[128,256]{1,0:T(8,128)S(1)}, u32[]{:S(2)}, u32[]{:S(2)}) collective-permute-start(f32[128,256]{1,0:T(8,128)S(1)} %get-tuple-element.129), channel_id=1, source_target_pairs={{0,15},{1,2},{2,1},{3,4},{4,3},{5,6},{6,5},{7,8},{8,7},{9,10},{10,... | collective-permute-start | bytes 393224 | tf_op jit(solution)/shard_map/ppermute | solution.py:271
  65.4 5.1 %collective-permute-start.14 = (f32[128,256]{1,0:T(8,128)S(1)}, f32[128,256]{1,0:T(8,128)S(1)}, u32[]{:S(2)}, u32[]{:S(2)}) collective-permute-start(f32[128,256]{1,0:T(8,128)S(1)} %sum.4.state_ref), channel_id=1, source_target_pairs={{0,64},{16,80},{32,96},{48,112},{64,128},{80,144},{96,160},{112,17... | collective-permute-start | bytes 393224 | tf_op jit(solution)/shard_map/ppermute | solution.py:268
  73.2 4.7 %collective-permute-start.16 = (f32[128,256]{1,0:T(8,128)S(1)}, f32[128,256]{1,0:T(8,128)S(1)}, u32[]{:S(2)}, u32[]{:S(2)}) collective-permute-start(f32[128,256]{1,0:T(8,128)S(1)} %get-tuple-element.131), channel_id=1, source_target_pairs={{0,15},{1,2},{2,1},{3,4},{4,3},{5,6},{6,5},{7,8},{8,7},{9,10},{10,... | collective-permute-start | bytes 393224 | tf_op jit(solution)/shard_map/ppermute | solution.py:271
  85.3 4.7 %collective-permute-start.20 = (f32[128,256]{1,0:T(8,128)S(1)}, f32[128,256]{1,0:T(8,128)S(1)}, u32[]{:S(2)}, u32[]{:S(2)}) collective-permute-start(f32[128,256]{1,0:T(8,128)S(1)} %get-tuple-element.141), channel_id=1, source_target_pairs={{0,15},{1,2},{2,1},{3,4},{4,3},{5,6},{6,5},{7,8},{8,7},{9,10},{10,... | collective-permute-start | bytes 393224 | tf_op jit(solution)/shard_map/ppermute | solution.py:271
  91.4 4.7 %collective-permute-start.22 = (f32[128,256]{1,0:T(8,128)S(1)}, f32[128,256]{1,0:T(8,128)S(1)}, u32[]{:S(2)}, u32[]{:S(2)}) collective-permute-start(f32[128,256]{1,0:T(8,128)S(1)} %get-tuple-element.146), channel_id=1, source_target_pairs={{0,15},{1,2},{2,1},{3,4},{4,3},{5,6},{6,5},{7,8},{8,7},{9,10},{10,... | collective-permute-start | bytes 393224 | tf_op jit(solution)/shard_map/ppermute | solution.py:271
  96.1 5.1 %collective-permute-start.23 = (f32[128,256]{1,0:T(8,128)S(1)}, f32[128,256]{1,0:T(8,128)S(1)}, u32[]{:S(2)}, u32[]{:S(2)}) collective-permute-start(f32[128,256]{1,0:T(8,128)S(1)} %sum.5.state_ref), channel_id=1, source_target_pairs={{0,64},{16,80},{32,96},{48,112},{64,128},{80,144},{96,160},{112,17... | collective-permute-start | bytes 393224 | tf_op jit(solution)/shard_map/ppermute | solution.py:268
  109.8 4.7 %collective-permute-start.27 = (f32[128,256]{1,0:T(8,128)S(1)}, f32[128,256]{1,0:T(8,128)S(1)}, u32[]{:S(2)}, u32[]{:S(2)}) collective-permute-start(f32[128,256]{1,0:T(8,128)S(1)} %get-tuple-element.153), channel_id=1, source_target_pairs={{0,15},{1,2},{2,1},{3,4},{4,3},{5,6},{6,5},{7,8},{8,7},{9,10},{10,... | collective-permute-start | bytes 393224 | tf_op jit(solution)/shard_map/ppermute | solution.py:271
  115.9 4.7 %collective-permute-start.29 = (f32[128,256]{1,0:T(8,128)S(1)}, f32[128,256]{1,0:T(8,128)S(1)}, u32[]{:S(2)}, u32[]{:S(2)}) collective-permute-start(f32[128,256]{1,0:T(8,128)S(1)} %get-tuple-element.158), channel_id=1, source_target_pairs={{0,15},{1,2},{2,1},{3,4},{4,3},{5,6},{6,5},{7,8},{8,7},{9,10},{10,... | collective-permute-start | bytes 393224 | tf_op jit(solution)/shard_map/ppermute | solution.py:271
  121.9 4.7 %collective-permute-start.31 = (f32[128,256]{1,0:T(8,128)S(1)}, f32[128,256]{1,0:T(8,128)S(1)}, u32[]{:S(2)}, u32[]{:S(2)}) collective-permute-start(f32[128,256]{1,0:T(8,128)S(1)} %get-tuple-element.163), channel_id=1, source_target_pairs={{0,15},{1,2},{2,1},{3,4},{4,3},{5,6},{6,5},{7,8},{8,7},{9,10},{10,... | collective-permute-start | bytes 393224 | tf_op jit(solution)/shard_map/ppermute | solution.py:271
  126.7 5.1 %collective-permute-start.32 = (f32[128,256]{1,0:T(8,128)S(1)}, f32[128,256]{1,0:T(8,128)S(1)}, u32[]{:S(2)}, u32[]{:S(2)}) collective-permute-start(f32[128,256]{1,0:T(8,128)S(1)} %sum.6.state_ref), channel_id=1, source_target_pairs={{0,64},{16,80},{32,96},{48,112},{64,128},{80,144},{96,160},{112,17... | collective-permute-start | bytes 393224 | tf_op jit(solution)/shard_map/ppermute | solution.py:268
  134.5 4.7 %collective-permute-start.34 = (f32[128,256]{1,0:T(8,128)S(1)}, f32[128,256]{1,0:T(8,128)S(1)}, u32[]{:S(2)}, u32[]{:S(2)}) collective-permute-start(f32[128,256]{1,0:T(8,128)S(1)} %get-tuple-element.165), channel_id=1, source_target_pairs={{0,15},{1,2},{2,1},{3,4},{4,3},{5,6},{6,5},{7,8},{8,7},{9,10},{10,... | collective-permute-start | bytes 393224 | tf_op jit(solution)/shard_map/ppermute | solution.py:271
  146.6 4.7 %collective-permute-start.38 = (f32[128,256]{1,0:T(8,128)S(1)}, f32[128,256]{1,0:T(8,128)S(1)}, u32[]{:S(2)}, u32[]{:S(2)}) collective-permute-start(f32[128,256]{1,0:T(8,128)S(1)} %get-tuple-element.175), channel_id=1, source_target_pairs={{0,15},{1,2},{2,1},{3,4},{4,3},{5,6},{6,5},{7,8},{8,7},{9,10},{10,... | collective-permute-start | bytes 393224 | tf_op jit(solution)/shard_map/ppermute | solution.py:271
  157.5 8.7 %collective-permute-start.41 = (f32[128,256]{1,0:T(8,128)S(1)}, f32[128,256]{1,0:T(8,128)S(1)}, u32[]{:S(2)}, u32[]{:S(2)}) collective-permute-start(f32[128,256]{1,0:T(8,128)S(1)} %get-tuple-element.182), channel_id=1, source_target_pairs={{0,16},{16,32},{32,48},{48,0},{64,80},{80,96},{96,112},{112,64},{1... | collective-permute-start | bytes 393224 | tf_op jit(solution)/shard_map/ppermute | solution.py:291
  157.6 8.6 %collective-permute-start.42 = (f32[128,256]{1,0:T(8,128)S(1)}, f32[128,256]{1,0:T(8,128)S(1)}, u32[]{:S(2)}, u32[]{:S(2)}) collective-permute-start(f32[128,256]{1,0:T(8,128)S(1)} %get-tuple-element.183), channel_id=1, source_target_pairs={{0,32},{16,48},{32,0},{48,16},{64,96},{80,112},{96,64},{112,80},{1... | collective-permute-start | bytes 393224 | tf_op jit(solution)/shard_map/ppermute | solution.py:291
  158.7 7.4 %collective-permute-start.43 = (f32[128,256]{1,0:T(8,128)S(1)}, f32[128,256]{1,0:T(8,128)S(1)}, u32[]{:S(2)}, u32[]{:S(2)}) collective-permute-start(f32[128,256]{1,0:T(8,128)S(1)} %get-tuple-element.184), channel_id=1, source_target_pairs={{0,48},{16,0},{32,16},{48,32},{64,112},{80,64},{96,80},{112,96},{1... | collective-permute-start | bytes 393224 | tf_op jit(solution)/shard_map/ppermute | solution.py:291
  (23 other events, 76.2 us)
